TPU v7x, 32 devices: a whole 2x2x4 slice. The times are simulated.
32 devices in a mesh: coarse: 4 (over x, core), fine: 8 (over z, y).
Axes of the slice: x: 2, y: 2, z: 4, core: 2. Of those that a mesh axis runs over, the one named last changes fastest.
Arguments:
- tokens: bfloat16 [16384, 1024], P(('coarse', 'fine'))
- w_qkv: bfloat16 [1024, 3072], replicated, may hold values from -0.1875 to 0.1875
- w_coarse_out: bfloat16 [1024, 1024], replicated, may hold values from -0.1875 to 0.1875
- w_kv2: bfloat16 [1024, 2048], replicated, may hold values from -0.1875 to 0.1875
- w_out: bfloat16 [1024, 1024], replicated, may hold values from -0.1875 to 0.1875
- seg_start: int32 [512], P('coarse'), may hold values from 0 to 16383, as said below
- seg_end: int32 [512], P('coarse'), may hold values from 1 to 16384, as said below
- block_lists: int32 [64, 8], P(('coarse', 'fine')), may hold values from 0 to 31, as said below
Outputs:
- mixed: bfloat16 [16384, 1024], P(('coarse', 'fine'))
Inputs may be any that keep to these rules, and one draw needn't show every extreme that they name: `seg_start`: for each coarse owner c, the segments c*128 to (c+1)*128 - 1 are nonempty and pairwise disjoint and lie within time steps c*4096 to (c+1)*4096 - 1, listed in an order that does not follow time; steps outside all segments belong to none; segment lengths are uneven. seg_end[s] > seg_start[s]. `block_lists`: row n names 8 distinct coarse key blocks (block b holds segments b*16 to (b+1)*16 - 1), all among the blocks of owners c-1, c and c+1 taken cyclically over the owners, where c = n*256 // 4096 is the owner of the row's time steps.
All inputs are finite; a program needn't handle non-finite values.
Results may differ from a plain program's by a relative error of at most 0.017.
Values may be sent and summed in bfloat16 or wider, within the bound.
No kernel may reach another device: no remote copies, remote signals or barrier semaphores. Data moves between devices by JAX's collectives and lax.ppermute only.
A program may use at most 128 MiB of HBM per device.

v0:
```python
import math

import jax
import jax.numpy as jnp
from jax import lax
from jax.sharding import PartitionSpec as P

HEADS = 8
KB = 16
QB = 256


def padded(cells, sides, width):
    for axis, dim in sides:
        count = lax.axis_size(axis)
        head = lax.slice_in_dim(cells, 0, width, axis=dim)
        tail = lax.slice_in_dim(cells, cells.shape[dim] - width, cells.shape[dim], axis=dim)
        cells = jnp.concatenate(
            [
                lax.ppermute(tail, axis, [(i, (i + 1) % count) for i in range(count)]),
                cells,
                lax.ppermute(head, axis, [((i + 1) % count, i) for i in range(count)]),
            ],
            axis=dim,
        )
    return cells


def attend_heads(queries, keys, content_elements, allowed):
    count = queries.shape[0]
    head_size = queries.shape[1] // HEADS
    query_heads = queries.reshape(count, HEADS, head_size)
    key_heads = keys.reshape(keys.shape[0], HEADS, head_size)
    value_heads = content_elements.reshape(content_elements.shape[0], HEADS, head_size)
    scores = jnp.einsum("qhd,khd->hqk", query_heads, key_heads, preferred_element_type=jnp.float32)
    scores = scores * (1.0 / math.sqrt(head_size))
    scores = jnp.where(allowed[None], scores, -1e30)
    highest = jnp.max(scores, axis=-1, keepdims=True)
    expos = jnp.exp(scores - highest)
    weights = (expos / jnp.sum(expos, axis=-1, keepdims=True)).astype(jnp.bfloat16)
    blended = jnp.einsum("hqk,khd->qhd", weights, value_heads, preferred_element_type=jnp.float32)
    return blended.astype(jnp.bfloat16).reshape(count, HEADS * head_size)


def normalize(content_elements):
    return content_elements * lax.rsqrt(
        jnp.mean(content_elements * content_elements, axis=-1, keepdims=True) + 1e-06
    )


def body(tokens, w_qkv, w_coarse_out, w_kv2, w_out, seg_start, seg_end, block_lists):
    rows_here = tokens.shape[0]
    width = tokens.shape[1]
    fine_count = lax.axis_size("fine")
    coarse_count = lax.axis_size("coarse")
    fine_index = lax.axis_index("fine")
    coarse_index = lax.axis_index("coarse")
    seg_owned = seg_start.shape[0]
    first_row = coarse_index * (rows_here * fine_count) + fine_index * rows_here
    positions = first_row + jnp.arange(rows_here, dtype=jnp.int32)
    member = (
        (positions[None, :] >= seg_start[:, None]) & (positions[None, :] < seg_end[:, None])
    ).astype(jnp.bfloat16)
    sums = lax.psum_scatter(
        jnp.dot(member, tokens, preferred_element_type=jnp.float32).astype(jnp.bfloat16),
        "fine",
        scatter_dimension=0,
        tiled=True,
    ).astype(jnp.float32)
    share_start = fine_index * KB
    spans = (
        lax.dynamic_slice_in_dim(seg_end, share_start, KB, 0)
        - lax.dynamic_slice_in_dim(seg_start, share_start, KB, 0)
    ).astype(jnp.float32)
    pooled = (sums / jnp.sqrt(spans)[:, None]).astype(jnp.bfloat16)
    coarse_proj = jnp.dot(pooled, w_qkv, preferred_element_type=jnp.float32)
    coarse_query = coarse_proj[:, :width].astype(jnp.bfloat16)
    coarse_pair = coarse_proj[:, width:].astype(jnp.bfloat16)
    owner_pairs = lax.all_gather(coarse_pair, "fine", axis=0, tiled=True)
    reach = seg_owned // 2
    window_table = padded(owner_pairs, (("coarse", 0),), reach)
    query_place = reach + share_start + jnp.arange(KB, dtype=jnp.int32)
    key_place = jnp.arange(window_table.shape[0], dtype=jnp.int32)
    allowed = jnp.abs(query_place[:, None] - key_place[None, :]) <= reach
    coarse_mix = attend_heads(
        coarse_query, window_table[:, :width], window_table[:, width:], allowed
    )
    context = jnp.dot(coarse_mix, w_coarse_out, preferred_element_type=jnp.float32)
    state = normalize(context).astype(jnp.bfloat16)
    payload = jnp.dot(state, w_kv2, preferred_element_type=jnp.float32).astype(jnp.bfloat16)
    seg_total = seg_owned * coarse_count
    owner_rows = lax.all_gather(payload, "fine", axis=0, tiled=True)
    second_table = padded(owner_rows, (("coarse", 0),), seg_owned)
    table_base = (coarse_index - 1) * seg_owned
    proj = jnp.dot(tokens, w_qkv, preferred_element_type=jnp.float32)
    query = proj[:, :width].astype(jnp.bfloat16)
    key_rows = proj[:, width : 2 * width].astype(jnp.bfloat16)
    value_rows = proj[:, 2 * width :].astype(jnp.bfloat16)
    listed_rows = (
        block_lists[:, :, None] * KB + jnp.arange(KB, dtype=jnp.int32)[None, None, :]
    ).reshape(block_lists.shape[0], -1)
    table_rows = jnp.mod(listed_rows - table_base, seg_total)
    block_rows = min(512, rows_here)
    sub_blocks = block_rows // QB
    remote_per_sub = table_rows.shape[1]
    query_group = jnp.arange(block_rows, dtype=jnp.int32) // QB
    remote_group = jnp.arange(sub_blocks * remote_per_sub, dtype=jnp.int32) // remote_per_sub
    allowed_fine = jnp.concatenate(
        [
            jnp.ones((block_rows, rows_here), dtype=bool),
            query_group[:, None] == remote_group[None, :],
        ],
        axis=1,
    )

    def query_block(number):
        wanted = table_rows.reshape(-1)
        remote = jnp.take(second_table, wanted, axis=0)
        keys = jnp.concatenate([key_rows, remote[:, :width]], axis=0)
        content_elements = jnp.concatenate([value_rows, remote[:, width:]], axis=0)
        return attend_heads(query, keys, content_elements, allowed_fine)

    attended = lax.map(query_block, jnp.arange(rows_here // block_rows, dtype=jnp.int32)).reshape(
        rows_here, width
    )
    projected = jnp.dot(attended, w_out, preferred_element_type=jnp.float32)
    return normalize(projected).astype(jnp.bfloat16)


def solution(mesh):
    placed = (
        P(("coarse", "fine"), None),
        P(),
        P(),
        P(),
        P(),
        P("coarse"),
        P("coarse"),
        P(("coarse", "fine"), None),
    )
    return jax.shard_map(
        body, mesh=mesh, in_specs=placed, out_specs=P(("coarse", "fine"), None), check_vma=False
    )
```

profile of v0, /device:TPU:0, one launch (start us, length us, event | category | flops | bytes accessed | tf_op | source)
XLA Modules:
  0.0 221.5 jit_solution(13709636266122746804)
XLA Ops:
  6.5 2.5 %convolution_convert_fusion.3 = bf16[128,1024]{1,0:T(8,128)(2,1)} fusion(bf16[512,1024]{1,0:T(8,128)(2,1)} %param.8, s32[512]{0:T(512)S(1)} %iota_add_fusion, s32[128]{0:T(128)} %param.14, s32[128]{0:T(128)} %param.13), kind=kOutput, calls=%fused_computation.23 | convolution fusion | flops 134545408 | bytes 1313792 | tf_op jit(solution)/shard_map/dot_general | solution.py:65
  9.0 0.8 convert_sqrt_fusion
  9.8 0.7 broadcast_multiply_fusion
  10.7 8.2 %convolution_convert_fusion = bf16[512,3072]{1,0:T(8,128)(2,1)} fusion(bf16[512,1024]{1,0:T(8,128)(2,1)} %param.8, bf16[1024,3072]{1,0:T(8,128)(2,1)} %param.9), kind=kOutput, calls=%fused_computation.11 | convolution fusion | flops 3222798336 | bytes 10485760 | tf_op jit(solution)/shard_map/dot_general | solution.py:95
  19.0 56.0 %reduce-scatter.2.cloned.1.call-done = bf16[16,1024]{1,0:T(8,128)(2,1)} async-done(((bf16[128,1024]{1,0:T(8,128)(2,1)}), bf16[16,1024]{1,0:T(8,128)(2,1)}) %reduce-scatter.2.cloned.1.call-update) | async-done | bytes 32784 | tf_op jit(solution)/shard_map/reduce_scatter | solution.py:64
  75.1 3.8 %convolution_convert_fusion.1 = bf16[16,3072]{1,0:T(8,128)(2,1)S(1)} fusion(bf16[1024,3072]{1,0:T(8,128)(2,1)} %param.9, bf16[16,1024]{1,0:T(8,128)(2,1)} %reduce-scatter.2.cloned.1.call-done, f32[16]{0:T(128)S(1)} %convert_sqrt_fusion), kind=kOutput, calls=%fused_computation.12 | convolution fusion | flops 100761600 | bytes 6422592 | tf_op jit(solution)/shard_map/dot_general | solution.py:76
  78.9 31.5 %all_gather.6 = bf16[128,2048]{1,0:T(8,128)(2,1)S(1)} all-gather(bf16[16,2048]{1,0:T(8,128)(2,1)S(1)} %slice.55), channel_id=1, replica_groups=mesh['coarse'=4,'fine'=8] {'fine'}, dimensions={0}, use_global_device_ids=true | all-gather | bytes 589824 | tf_op jit(solution)/shard_map/all_gather | solution.py:79
  110.7 1.8 collective-permute-start.1
  112.4 4.8 %collective-permute-done = bf16[64,2048]{1,0:T(8,128)(2,1)S(1)} collective-permute-done((bf16[64,2048]{1,0:T(8,128)(2,1)S(1)}, bf16[64,2048]{1,0:T(8,128)(2,1)S(1)}, u32[]{:S(2)}, u32[]{:S(2)}) %collective-permute-start) | collective-permute-done | bytes 262176 | tf_op jit(solution)/shard_map/ppermute | solution.py:20
  117.3 0.7 collective-permute-done.1
  118.1 0.4 fusion.45
  118.5 0.2 fusion.14
  118.7 2.1 multiply_reduce_fusion.1
  120.8 2.9 %convolution_convert_fusion.2 = bf16[16,2048]{1,0:T(8,128)(2,1)S(1)} fusion(bf16[1024,2048]{1,0:T(8,128)(2,1)} %param.11, f32[16,1024]{1,0:T(8,128)S(1)} %get-tuple-element.41, f32[16]{0:T(128)S(1)} %add_rsqrt_fusion.1), kind=kOutput, calls=%fused_computation.13 | convolution fusion | flops 67174400 | bytes 4325440 | tf_op jit(solution)/shard_map/dot_general | solution.py:90
  123.7 31.6 %all_gather.7 = bf16[128,2048]{1,0:T(8,128)(2,1)S(1)} all-gather(bf16[16,2048]{1,0:T(8,128)(2,1)S(1)} %convolution_convert_fusion.2), channel_id=1, replica_groups=mesh['coarse'=4,'fine'=8] {'fine'}, dimensions={0}, use_global_device_ids=true | all-gather | bytes 589824 | tf_op jit(solution)/shard_map/all_gather | solution.py:92
  155.3 0.5 collective-permute-start.2
  155.9 0.8 concatenate.20
  156.7 3.6 %slice_bitcast_fusion = (bf16[64,8,8,128]{3,2,1,0:T(8,128)(2,1)}, bf16[512,1024]{1,0:T(8,128)(2,1)}, bf16[512,1024]{1,0:T(8,128)(2,1)}) fusion(bf16[512,3072]{1,0:T(8,128)(2,1)} %convolution_convert_fusion), kind=kLoop, calls=%fused_computation.32 | loop fusion | bytes 6291456
  160.3 6.5 %collective-permute-done.3 = bf16[128,2048]{1,0:T(8,128)(2,1)S(1)} collective-permute-done((bf16[128,2048]{1,0:T(8,128)(2,1)S(1)}, bf16[128,2048]{1,0:T(8,128)(2,1)S(1)}, u32[]{:S(2)}, u32[]{:S(2)}) %collective-permute-start.3) | collective-permute-done | bytes 524320 | tf_op jit(solution)/shard_map/ppermute | solution.py:22
  166.8 2.8 %collective-permute-done.2 = bf16[128,2048]{1,0:T(8,128)(2,1)} collective-permute-done((bf16[128,2048]{1,0:T(8,128)(2,1)S(1)}, bf16[128,2048]{1,0:T(8,128)(2,1)}, u32[]{:S(2)}, u32[]{:S(2)}) %collective-permute-start.2) | collective-permute-done | bytes 524320 | tf_op jit(solution)/shard_map/ppermute | solution.py:20
  169.6 2.3 %pad_maximum_fusion = bf16[384,2048]{1,0:T(8,128)(2,1)} fusion(bf16[128,2048]{1,0:T(8,128)(2,1)S(1)} %collective-permute-done.3, bf16[128,2048]{1,0:T(8,128)(2,1)S(1)} %all_gather.7, bf16[128,2048]{1,0:T(8,128)(2,1)} %collective-permute-done.2), kind=kLoop, calls=%fused_computation.19 | loop fusion | flops 4718592 | bytes 3145728 | tf_op jit(solution)/shard_map/concatenate | solution.py:18
  171.9 4.0 %gather_fusion = bf16[256,2048]{1,0:T(8,128)(2,1)S(1)} fusion(bf16[384,2048]{1,0:T(8,128)(2,1)} %pad_maximum_fusion, s32[1024]{0:T(1024)S(1)} %pad_clamp_fusion), kind=kCustom, calls=%fused_computation | custom fusion | bytes 2098176 | tf_op jit(solution)/shard_map/while/body/eval_jaxpr/jit(_take)/gather | solution.py:118
  175.9 0.2 broadcast_select_fusion
  176.0 0.9 fusion.43
  176.9 0.3 copy-done.1
  177.2 1.3 pad_maximum_fusion.1
  178.5 2.6 %copy.22 = bf16[768,1024]{0,1:T(8,128)(2,1)} copy(bf16[768,1024]{1,0:T(8,128)(2,1)} %pad_maximum_fusion.1) | data formatting | bytes 3145728 | tf_op jit(solution)/shard_map/while/body/eval_jaxpr/reshape | solution.py:34
  181.1 7.8 %fusion.7 = f32[8,512,768]{2,1,0:T(8,128)} fusion(bf16[64,8,8,128]{3,2,1,0:T(8,128)(2,1)S(1)} %copy-done.2, bf16[256,1024]{1,0:T(8,128)(2,1)} %get-tuple-element.22, bf16[512,1024]{1,0:T(8,128)(2,1)} %get-tuple-element.20), kind=kOutput, calls=%fused_computation.16 | convolution fusion | flops 808452096 | bytes 15204352 | tf_op jit(solution)/shard_map/while/body/eval_jaxpr/qhd,khd->hqk/dot_general | solution.py:35
  189.0 16.2 %fusion.46 = (f32[8,512]{1,0:T(8,128)S(1)}, f32[8,512,768]{2,1,0:T(8,128)}) fusion(f32[8,512,768]{2,1,0:T(8,128)} %fusion.7, pred[512,768]{1,0:T(8,128)(4,1)S(1)} %copy-done.4), kind=kOutput, calls=%fused_computation.100 | output fusion | flops 18875136 | bytes 25575424 | tf_op jit(solution)/shard_map/while/body/eval_jaxpr/sub | solution.py:39
  205.2 6.9 %fusion.10 = bf16[8,128,512]{2,1,0:T(8,128)(2,1)S(1)} fusion(bf16[768,8,128]{0,2,1:T(8,128)(2,1)S(1)} %bitcast.65, f32[8,512,768]{2,1,0:T(8,128)} %get-tuple-element.43, f32[8,512]{1,0:T(8,128)S(1)} %get-tuple-element.42), kind=kOutput, calls=%fused_computation.22 | convolution fusion | flops 812122112 | bytes 15220736 | tf_op jit(solution)/shard_map/while/body/eval_jaxpr/hqk,khd->qhd/dot_general | solution.py:41
  212.1 1.4 multiply_reduce_fusion
  213.5 1.2 multiply_convert_fusion
  (36 shorter events, 0.9 us)
Async XLA Ops:
  6.5 205.5 %copy-start = (bf16[1024,1024]{1,0:T(8,128)(2,1)S(1)}, bf16[1024,1024]{1,0:T(8,128)(2,1)}, u32[]{:S(2)}) copy-start(bf16[1024,1024]{1,0:T(8,128)(2,1)} %param.12) | copy-start | bytes 6291460
  6.5 68.5 %reduce-scatter.2.cloned.1.call-start = ((), (), s32[]{:S(2)}) async-start(), calls=%async_computation.1 | async-start | bytes 294912 | tf_op jit(solution)/shard_map/reduce_scatter | solution.py:64
  110.4 6.8 %collective-permute-start = (bf16[64,2048]{1,0:T(8,128)(2,1)S(1)}, bf16[64,2048]{1,0:T(8,128)(2,1)S(1)}, u32[]{:S(2)}, u32[]{:S(2)}) collective-permute-start(bf16[64,2048]{1,0:T(8,128)(2,1)S(1)} %get-tuple-element.37), channel_id=1, source_target_pairs={{0,8},{8,16},{16,24},{24,0},{1,9},{9,17},{17,25},{25,1},{2,10},{10... | collective-permute-start | bytes 786440 | tf_op jit(solution)/shard_map/ppermute | solution.py:20
  110.7 7.3 %collective-permute-start.1 = (bf16[64,2048]{1,0:T(8,128)(2,1)S(1)}, bf16[64,2048]{1,0:T(8,128)(2,1)S(1)}, u32[]{:S(2)}, u32[]{:S(2)}) collective-permute-start(bf16[64,2048]{1,0:T(8,128)(2,1)S(1)} %get-tuple-element.36), channel_id=1, source_target_pairs={{8,0},{16,8},{24,16},{0,24},{9,1},{17,9},{25,17},{1,25},{10,2},{18... | collective-permute-start | bytes 786440 | tf_op jit(solution)/shard_map/ppermute | solution.py:22
  155.3 11.5 %collective-permute-start.3 = (bf16[128,2048]{1,0:T(8,128)(2,1)S(1)}, bf16[128,2048]{1,0:T(8,128)(2,1)S(1)}, u32[]{:S(2)}, u32[]{:S(2)}) collective-permute-start(bf16[128,2048]{1,0:T(8,128)(2,1)S(1)} %all_gather.7), channel_id=1, source_target_pairs={{8,0},{16,8},{24,16},{0,24},{9,1},{17,9},{25,17},{1,25},{10,2},{18... | collective-permute-start | bytes 1572872 | tf_op jit(solution)/shard_map/ppermute | solution.py:22
  155.3 14.3 %collective-permute-start.2 = (bf16[128,2048]{1,0:T(8,128)(2,1)S(1)}, bf16[128,2048]{1,0:T(8,128)(2,1)}, u32[]{:S(2)}, u32[]{:S(2)}) collective-permute-start(bf16[128,2048]{1,0:T(8,128)(2,1)S(1)} %all_gather.7), channel_id=1, source_target_pairs={{0,8},{8,16},{16,24},{24,0},{1,9},{9,17},{17,25},{25,1},{2,10},{10... | collective-permute-start | bytes 1572872 | tf_op jit(solution)/shard_map/ppermute | solution.py:20
  175.9 1.3 copy-start.1
  177.2 3.9 %copy-start.2 = (bf16[64,8,8,128]{3,2,1,0:T(8,128)(2,1)S(1)}, bf16[64,8,8,128]{3,2,1,0:T(8,128)(2,1)}, u32[]{:S(2)}) copy-start(bf16[64,8,8,128]{3,2,1,0:T(8,128)(2,1)} %get-tuple-element.19) | copy-start | bytes 3145732
  181.1 7.8 %copy-start.4 = (pred[512,768]{1,0:T(8,128)(4,1)S(1)}, pred[512,768]{1,0:T(8,128)(4,1)}, u32[]{:S(2)}) copy-start(pred[512,768]{1,0:T(8,128)(4,1)} %concatenate.20) | copy-start | bytes 1179652
  189.0 16.2 %copy-start.3 = (bf16[768,1024]{0,1:T(8,128)(2,1)S(1)}, bf16[768,1024]{0,1:T(8,128)(2,1)}, u32[]{:S(2)}) copy-start(bf16[768,1024]{0,1:T(8,128)(2,1)} %copy.22) | copy-start | bytes 4718596
Sparse Core Ops, SparseCore 0:
  10.7 64.3 reduce-scatter.1
where the time goes:
time: 222 us; the launch traced here: 221 us
  waiting for transfers between devices  70.7 us (32%)
  blocking collectives  63.1 us (28%)
  matrix products  36.1 us (16%)
  other arithmetic  22.9 us (10%)
  between operations  13.5 us (6%)
  local copies, waits for them, and re-layouts  12.7 us (6%)
  starting transfers between devices  2.35 us (1%)
    reduce_scatter x1, waiting for transfers between devices, body(): lax.psum_scatter(jnp.dot(member, tokens, preferred_element_type=jnp.float...  56 us
    all_gather x1, blocking collectives, body(): owner_rows = lax.all_gather(payload, 'fine', axis=0, tiled=True)  31.6 us
    all_gather x1, blocking collectives, body(): owner_pairs = lax.all_gather(coarse_pair, 'fine', axis=0, tiled=True)  31.5 us
    sub x1, other arithmetic, attend_heads(): expos = jnp.exp(scores - highest)  16.2 us
    dot_general x1, matrix products, body(): proj = jnp.dot(tokens, w_qkv, preferred_element_type=jnp.float32)  8.22 us
    dot_general x1, matrix products, attend_heads(): jnp.einsum('qhd,khd->hqk', query_heads, key_heads, preferred_element_type...  7.82 us
    ppermute x2, waiting for transfers between devices, padded(): lax.ppermute(tail, axis, [(i, (i + 1) % count) for i in range(count)])  7.52 us
    ppermute x2, waiting for transfers between devices, padded(): lax.ppermute(head, axis, [((i + 1) % count, i) for i in range(count)])  7.14 us
  transfers between devices with their start and end apart: 5, of which 5 were waited for; matrix products, arithmetic and copies ran while one was open for 7% of the time, Pallas kernels for 0%

commit v1 on v0

v1 whole, which is shorter than its diff:
```python
import functools
import math

import jax
import jax.numpy as jnp
from jax import lax
from jax.experimental import pallas as pl
from jax.experimental.pallas import tpu as pltpu
from jax.sharding import PartitionSpec as P

HEADS = 8
KB = 16
QB = 256
BLK = 128
MIB = 1 << 20
AXES = ("coarse", "fine")
F32 = jnp.float32
BF16 = jnp.bfloat16

VM = pl.BlockSpec(memory_space=pltpu.VMEM)
SM = pl.BlockSpec(memory_space=pltpu.SMEM)


def cdiv(a, b):
    return -(-a // b)


def dot(a, b):
    return jnp.dot(a, b, preferred_element_type=F32)


def dot_t(a, b):
    return lax.dot_general(a, b, (((1,), (1,)), ((), ())), preferred_element_type=F32)


def call(kernel, outs, in_specs, scratch, limit, flops, moved, name):
    return pl.pallas_call(
        kernel,
        out_shape=outs,
        in_specs=in_specs,
        out_specs=jax.tree.map(lambda _: VM, outs),
        scratch_shapes=scratch,
        compiler_params=pltpu.CompilerParams(vmem_limit_bytes=limit * MIB),
        cost_estimate=pl.CostEstimate(flops=flops, bytes_accessed=moved, transcendentals=0),
        name=name,
    )


def sums_kernel(chunk, place, starts, ends, tokens, own, send, acc):
    rows = tokens.shape[0]
    owned = starts.shape[1]
    mine = place[0]
    first = place[1]
    where_ = first + lax.broadcasted_iota(jnp.int32, (BLK, rows), 1)
    for s in range(owned // BLK):
        at = slice(s * BLK, (s + 1) * BLK)
        low = jnp.broadcast_to(starts[:, at], (BLK, BLK)).T
        high = jnp.broadcast_to(ends[:, at], (BLK, BLK)).T
        low = jnp.concatenate([low] * (rows // BLK), axis=1)
        high = jnp.concatenate([high] * (rows // BLK), axis=1)
        member = jnp.where((where_ >= low) & (where_ < high), 1.0, 0.0).astype(BF16)
        acc[at, :] = dot(member, tokens[...])
    own[...] = acc[pl.ds(pl.multiple_of(mine * chunk, chunk), chunk), :]
    for r in range(1, 4):
        theirs = pl.multiple_of((mine ^ r) * chunk, chunk)
        send[r - 1] = acc[pl.ds(theirs, chunk), :].astype(BF16)


def local_kernel(first, heads, size, scale, tokens, w_qkv, query, mix, level):
    width = tokens.shape[1]
    span = heads * size
    parts = []
    for k in range(3):
        at = k * width + first * size
        parts.append(dot(tokens[...], w_qkv[:, at : at + span]).astype(BF16))
    queries, keys, cells = parts
    query[...] = queries
    ones = jnp.ones((keys.shape[0], size), BF16)
    for i in range(heads):
        at = slice(i * size, (i + 1) * size)
        scores = dot_t(queries[:, at], keys[:, at])
        highest = jnp.max(scores, axis=1, keepdims=True)
        expos = jnp.exp2((scores - highest) * scale).astype(BF16)
        both = dot(expos, jnp.concatenate([cells[:, at], ones], axis=1))
        total = both[:, size:]
        mix[:, at] = both[:, :size] / total
        level[:, at] = highest * scale + jnp.log2(total)


def normalize_rows(source, target):
    def step(i, carry):
        at = pl.ds(pl.multiple_of(i * BLK, BLK), BLK)
        cells = source[at, :]
        level = jnp.mean(cells * cells, axis=1, keepdims=True)
        target[at, :] = (cells * lax.rsqrt(level + 1e-06)).astype(BF16)
        return carry

    lax.fori_loop(0, source.shape[0] // BLK, step, 0)


def matmul_into(target, source, weight, first, count, tile):
    def step(i, carry):
        to = pl.ds(pl.multiple_of(i * tile, tile), tile)
        of = pl.ds(pl.multiple_of(first + i * tile, tile), tile)
        target[:, to] = dot(source[...], weight[:, of]).astype(target.dtype)
        return carry

    lax.fori_loop(0, count // tile, step, 0)


def final_kernel(
    chunk, reach, size, scale, total_rows, group,
    place, lists, own0, own1, before0, before1, after0, after1, pair0, pair1, side0, side1,
    w_qkv, w_co, w_kv2, w_out, *rest,
):
    parts = len(rest) - 8
    query, mix, level = (rest[k:parts:3] for k in range(3))
    out, table, halo, pairs, coarse, wide, listed, second = rest[parts:]
    width = table.shape[1]
    owned = chunk * 4
    mine = place[0]
    core = place[2]
    owner = place[3]

    def lay(base, zero, one):
        for r in range(4):
            to = pl.multiple_of(base + (mine ^ r) * chunk, chunk)
            source = one if r & 1 else zero
            table[pl.ds(to, chunk), :] = source[(r >> 1) * chunk : (r >> 1) * chunk + chunk, :]

    def lay_halo(zero, one, first, to):
        for r in range(4):
            at = pl.multiple_of((mine ^ r) * chunk, chunk)
            source = one if r & 1 else zero
            halo[pl.ds(at, chunk), :] = source[(r >> 1) * chunk : (r >> 1) * chunk + chunk, :]
        table[to : to + reach, :] = halo[first : first + reach, :]

    lay_halo(before0, before1, owned - reach, 0)
    lay_halo(after0, after1, 0, reach + 3 * owned)
    lay(reach + owned, own0, own1)
    lay(reach + (1 - core) * 2 * owned, pair0, pair1)
    lay(reach + core * 2 * owned, side0, side1)

    matmul_into(pairs, table, w_qkv, width, 2 * width, 512)
    matmul_into(coarse, table.at[pl.ds(reach, 3 * owned)], w_qkv, 0, width, 512)

    span = BLK + 2 * reach
    row = lax.broadcasted_iota(jnp.int32, (BLK, span), 0)
    column = lax.broadcasted_iota(jnp.int32, (BLK, span), 1)
    inside = (column >= row) & (column <= row + 2 * reach)
    ones = jnp.ones((span, size), BF16)

    def coarse_step(i, carry):
        first = pl.multiple_of(i * BLK, BLK)
        for h in range(HEADS):
            at = slice(h * size, (h + 1) * size)
            keys = pairs[pl.ds(first, span), at]
            cells = pairs[pl.ds(first, span), width + h * size : width + (h + 1) * size]
            scores = jnp.where(inside, dot_t(coarse[pl.ds(first, BLK), at], keys), -1e30)
            highest = jnp.max(scores, axis=1, keepdims=True)
            expos = jnp.exp2((scores - highest) * scale).astype(BF16)
            both = dot(expos, jnp.concatenate([cells, ones], axis=1))
            coarse[pl.ds(first, BLK), at] = (both[:, :size] / both[:, size:]).astype(BF16)
        return carry

    lax.fori_loop(0, 3 * owned // BLK, coarse_step, 0)
    matmul_into(wide.at[pl.ds(0, 3 * owned)], coarse, w_co, 0, width, 512)
    normalize_rows(wide.at[pl.ds(0, 3 * owned)], coarse)

    base = (owner - 1) * owned
    groups, picks = lists.shape
    for n in range(groups):
        for m in range(picks):
            at = lax.rem(lists[n, m] * KB - base + total_rows, total_rows)
            to = (n * picks + m) * KB
            listed[to : to + KB, :] = coarse[pl.ds(pl.multiple_of(at, KB), KB), :]
    matmul_into(second, listed, w_kv2, 0, 2 * width, 512)

    here = picks * KB
    ones_here = jnp.ones((here, size), BF16)
    for n in range(groups):
        rows = slice(n * QB, (n + 1) * QB)
        theirs = slice(n * here, (n + 1) * here)
        for h in range(HEADS):
            at = slice(h * size, (h + 1) * size)
            part, where_ = h // group, slice(h % group * size, (h % group + 1) * size)
            scores = dot_t(query[part][rows, where_], second[theirs, at]) * scale
            before = level[part][rows, where_]
            highest = jnp.maximum(before, jnp.max(scores, axis=1, keepdims=True))
            expos = jnp.exp2(scores - highest[:, :here]).astype(BF16)
            cells = second[theirs, width + h * size : width + (h + 1) * size]
            both = dot(expos, jnp.concatenate([cells, ones_here], axis=1))
            keep = jnp.exp2(before - highest)
            mixed = mix[part][rows, where_] * keep + both[:, :size]
            out[rows, at] = (mixed / (keep + both[:, size:])).astype(BF16)
    rows_here = out.shape[0]
    matmul_into(wide.at[pl.ds(0, rows_here)], out, w_out, 0, width, 512)
    normalize_rows(wide.at[pl.ds(0, rows_here)], out)


def swap(cells, coarse_bit, fine_bit):
    coarse_count = lax.axis_size("coarse")
    fine_count = lax.axis_size("fine")
    pairs = [
        (c * fine_count + f, (c ^ coarse_bit) * fine_count + (f ^ fine_bit))
        for c in range(coarse_count)
        for f in range(fine_count)
    ]
    return lax.ppermute(cells, AXES, pairs)


def shift(cells, chips, fine_bit):
    coarse_count = lax.axis_size("coarse")
    fine_count = lax.axis_size("fine")
    pairs = [
        (c * fine_count + f, ((c + 2 * chips) % coarse_count) * fine_count + (f ^ fine_bit))
        for c in range(coarse_count)
        for f in range(fine_count)
    ]
    return lax.ppermute(cells, AXES, pairs)


def body(tokens, w_qkv, w_coarse_out, w_kv2, w_out, seg_start, seg_end, block_lists):
    rows_here, width = tokens.shape
    size = width // HEADS
    fine_count = lax.axis_size("fine")
    coarse_count = lax.axis_size("coarse")
    fine_index = lax.axis_index("fine")
    coarse_index = lax.axis_index("coarse")
    owned = seg_start.shape[0]
    chunk = owned // 4
    reach = owned // 2
    scale = math.log2(math.e) / math.sqrt(size)
    mine = fine_index & 3
    big = coarse_count > 4
    if not big:
        tokens, w_qkv, w_coarse_out, w_kv2, w_out = (
            pltpu.with_memory_space_constraint(c, pltpu.VMEM)
            for c in (tokens, w_qkv, w_coarse_out, w_kv2, w_out)
        )
    first_row = coarse_index * (rows_here * fine_count) + fine_index * rows_here
    place = jnp.stack([mine, first_row, coarse_index & 1, coarse_index]).astype(jnp.int32)

    own, send = call(
        functools.partial(sums_kernel, chunk),
        (
            jax.ShapeDtypeStruct((chunk, width), F32),
            jax.ShapeDtypeStruct((3, chunk, width), BF16),
        ),
        [SM, VM, VM, VM],
        [pltpu.VMEM((owned, width), F32)],
        16,
        2 * owned * rows_here * width,
        rows_here * width * 2,
        "sums",
    )(place, seg_start.reshape(1, owned), seg_end.reshape(1, owned), tokens)

    group = 2

    def local(first):
        span = group * size
        return call(
            functools.partial(local_kernel, first, group, size, scale),
            (
                jax.ShapeDtypeStruct((rows_here, span), BF16),
                jax.ShapeDtypeStruct((rows_here, span), F32),
                jax.ShapeDtypeStruct((rows_here, span), F32),
            ),
            [VM, VM],
            [],
            32 if big else 16,
            2 * rows_here * width * 3 * span,
            width * 3 * span * 2,
            f"local{first}",
        )(tokens, w_qkv)

    parts = [part for first in range(0, HEADS, group) for part in local(first)]

    spans = (
        lax.dynamic_slice_in_dim(seg_end, mine * chunk, chunk, 0)
        - lax.dynamic_slice_in_dim(seg_start, mine * chunk, chunk, 0)
    ).astype(F32)
    roots = jnp.sqrt(spans)[:, None]

    got = [swap(send[r - 1], 0, r) for r in range(1, 4)]
    sums = own + got[0].astype(F32) + got[1].astype(F32) + got[2].astype(F32)
    bit = 4
    while bit < fine_count:
        sums = sums + swap(sums.astype(BF16), 0, bit).astype(F32)
        bit *= 2
    pooled = (sums / roots).astype(BF16)
    own0 = jnp.concatenate([pooled, swap(pooled, 0, 2)], axis=0)
    own1 = swap(own0, 0, 1)
    chips = coarse_count // 2
    core = coarse_index & 1
    if chips == 2:
        before0 = after0 = side0 = swap(own0, 2, 0)
        before1 = after1 = side1 = swap(own0, 2, 1)
    else:
        before0, before1 = shift(own0, 1, 0), shift(own0, 1, 1)
        after0, after1 = shift(own0, -1, 0), shift(own0, -1, 1)
        side0 = jnp.where(core == 0, after0, before0)
        side1 = jnp.where(core == 0, after1, before1)
    pair0, pair1, side0, side1 = (swap(c, 1, 0) for c in (own0, own1, side0, side1))

    table_rows = 3 * owned + 2 * reach
    listed_rows = block_lists.shape[0] * block_lists.shape[1] * KB
    wide_rows = max(rows_here, 3 * owned)
    return call(
        functools.partial(final_kernel, chunk, reach, size, scale, owned * coarse_count, group),
        jax.ShapeDtypeStruct((rows_here, width), BF16),
        [SM, SM] + [VM] * (14 + len(parts)),
        [
            pltpu.VMEM((table_rows, width), BF16),
            pltpu.VMEM((owned, width), BF16),
            pltpu.VMEM((table_rows, 2 * width), BF16),
            pltpu.VMEM((3 * owned, width), BF16),
            pltpu.VMEM((wide_rows, width), F32),
            pltpu.VMEM((listed_rows, width), BF16),
            pltpu.VMEM((listed_rows, 2 * width), BF16),
        ],
        60 if big else 20,
        2 * table_rows * width * 3 * width,
        0,
        "final",
    )(
        place, block_lists, own0, own1, before0, before1, after0, after1, pair0, pair1, side0, side1,
        w_qkv, w_coarse_out, w_kv2, w_out, *parts,
    )


def solution(mesh):
    placed = (
        P(("coarse", "fine"), None),
        P(),
        P(),
        P(),
        P(),
        P("coarse"),
        P("coarse"),
        P(("coarse", "fine"), None),
    )
    return jax.shard_map(
        body, mesh=mesh, in_specs=placed, out_specs=P(("coarse", "fine"), None), check_vma=False
    )
```

time: 222 us -> 56.4 us (0.25)
  blocking collectives: 63.1 us -> 0 us
  waiting for transfers between devices: 70.7 us -> 10.7 us
  matrix products: 36.1 us -> 0 us
  Pallas kernels: 0 us -> 24.7 us
  other arithmetic: 22.9 us -> 0.95 us
  between operations: 13.5 us -> 0.19 us
  starting transfers between devices: 2.35 us -> 12.3 us
  local copies, waits for them, and re-layouts: 12.7 us -> 7.32 us
    all_gather x2 -> x0, blocking collectives: 63.1 us -> none  [the longest x1 31.6 us: body(): owner_rows = lax.all_gather(payload, 'fine', axis=0, tiled=True)]
    reduce_scatter x1 -> x0, waiting for transfers between devices: 56 us -> none  [body(): lax.psum_scatter(jnp.dot(member, tokens, preferred_element_type=jnp.float...]
    dot_general x9 -> x0, matrix products: 35.7 us -> none  [the longest x1 8.22 us: body(): proj = jnp.dot(tokens, w_qkv, preferred_element_type=jnp.float32)]
    pallas_call x0 -> x6, Pallas kernels: none -> 24.7 us  [the longest x1 15.7 us: body(): call(functools.partial(final_kernel, chunk, reach, size, scale, owned * c...]
    sub x1 -> x0, other arithmetic: 16.2 us -> none  [attend_heads(): expos = jnp.exp(scores - highest)]
    ppermute x4 -> x12, starting transfers between devices: 2.35 us -> 12.3 us  [swap(): return lax.ppermute(cells, AXES, pairs)]
    ppermute x4 -> x12, waiting for transfers between devices: 14.7 us -> 10.7 us  [swap(): return lax.ppermute(cells, AXES, pairs)]
    gather x1 -> x0, local copies, waits for them, and re-layouts: 3.97 us -> none  [query_block(): remote = jnp.take(second_table, wanted, axis=0)]
  transfers between devices with their start and end apart: 5 -> 12, of which waited for: 5 -> 4; matrix products, arithmetic and copies ran while one was open for 7% -> 1% of each run, Pallas kernels for 0% -> 14%
where the time goes in v1:
time: 56.4 us; the launch traced here: 56.2 us
  Pallas kernels  24.7 us (44%)
  starting transfers between devices  12.3 us (22%)
  waiting for transfers between devices  10.7 us (19%)
  local copies, waits for them, and re-layouts  7.32 us (13%)
  other arithmetic  0.95 us (2%)
    pallas_call x1, Pallas kernels, body(): call(functools.partial(final_kernel, chunk, reach, size, scale, owned * c...  15.7 us
    ppermute x12, starting transfers between devices, swap(): return lax.ppermute(cells, AXES, pairs)  12.3 us
    ppermute x12, waiting for transfers between devices, swap(): return lax.ppermute(cells, AXES, pairs)  10.7 us
    pallas_call x4, Pallas kernels, local(): call(functools.partial(local_kernel, first, group, size, scale), (jax.Sha...  8.11 us
    unnamed x22, local copies, waits for them, and re-layouts  7.31 us
  transfers between devices with their start and end apart: 12, of which 4 were waited for; matrix products, arithmetic and copies ran while one was open for 1% of the time, Pallas kernels for 14%

profile of v1, /device:TPU:0, one launch (start us, length us, event | category | flops | bytes accessed | tf_op | source)
XLA Modules:
  0.0 56.2 jit_solution(460711876131717383)
XLA Ops:
  0.0 0.1 pad_add_fusion.place
  0.1 1.2 %copy-done.1 = bf16[512,1024]{1,0:T(8,128)(2,1)S(1)} copy-done((bf16[512,1024]{1,0:T(8,128)(2,1)S(1)}, bf16[512,1024]{1,0:T(8,128)(2,1)}, u32[]{:S(2)}) %copy-start.1) | copy-done | bytes 1048600
  1.3 0.7 %copy-done.6 = s32[128]{0:T(128)S(1)} copy-done((s32[128]{0:T(128)S(1)}, s32[128]{0:T(128)}, u32[]{:S(2)}) %copy-start.6) | copy-done | bytes 536
  2.0 0.7 %copy-done.7 = s32[128]{0:T(128)S(1)} copy-done((s32[128]{0:T(128)S(1)}, s32[128]{0:T(128)}, u32[]{:S(2)}) %copy-start.7) | copy-done | bytes 536
  2.6 0.9 %sums.1 = (f32[32,1024]{1,0:T(8,128)S(1)}, bf16[3,32,1024]{2,1,0:T(8,128)(2,1)S(1)}) custom-call(s32[4]{0:T(128)S(1)} %pad_add_fusion.place, s32[1,128]{1,0:T(1,128)S(1)} %bitcast.14, s32[1,128]{1,0:T(1,128)S(1)} %bitcast.15, bf16[512,1024]{1,0:T(8,128)(2,1)S(1)} %copy-done.1), custom_call_target="tpu_custom_call" | custom-call | flops 134217728 | bytes 1048576 | tf_op jit(solution)/shard_map/sums/pallas_call | solution.py:244
  3.6 3.0 %collective-permute-start = (bf16[32,1024]{1,0:T(8,128)(2,1)S(1)}, bf16[32,1024]{1,0:T(8,128)(2,1)S(1)}, u32[]{:S(2)}, u32[]{:S(2)}) collective-permute-start(bf16[32,1024]{1,0:T(8,128)(2,1)S(1)} %get-tuple-element.33), channel_id=1, source_target_pairs={{0,1},{1,0},{2,3},{3,2},{4,5},{5,4},{6,7},{7,6},{8,9},{9,8},{10,11... | collective-permute-start | bytes 196616 | tf_op jit(solution)/shard_map/ppermute | solution.py:209
  6.6 1.5 %collective-permute-start.2 = (bf16[32,1024]{1,0:T(8,128)(2,1)S(1)}, bf16[32,1024]{1,0:T(8,128)(2,1)S(1)}, u32[]{:S(2)}, u32[]{:S(2)}) collective-permute-start(bf16[32,1024]{1,0:T(8,128)(2,1)S(1)} %get-tuple-element.34), channel_id=1, source_target_pairs={{0,3},{1,2},{2,1},{3,0},{4,7},{5,6},{6,5},{7,4},{8,11},{9,10},{10,... | collective-permute-start | bytes 196616 | tf_op jit(solution)/shard_map/ppermute | solution.py:209
  8.1 0.1 collective-permute-start.1
  8.2 1.2 %collective-permute-done = bf16[32,1024]{1,0:T(8,128)(2,1)S(1)} collective-permute-done((bf16[32,1024]{1,0:T(8,128)(2,1)S(1)}, bf16[32,1024]{1,0:T(8,128)(2,1)S(1)}, u32[]{:S(2)}, u32[]{:S(2)}) %collective-permute-start) | collective-permute-done | bytes 65568 | tf_op jit(solution)/shard_map/ppermute | solution.py:209
  9.4 3.0 %collective-permute-done.2 = bf16[32,1024]{1,0:T(8,128)(2,1)S(1)} collective-permute-done((bf16[32,1024]{1,0:T(8,128)(2,1)S(1)}, bf16[32,1024]{1,0:T(8,128)(2,1)S(1)}, u32[]{:S(2)}, u32[]{:S(2)}) %collective-permute-start.2) | collective-permute-done | bytes 65568 | tf_op jit(solution)/shard_map/ppermute | solution.py:209
  12.4 2.7 %collective-permute-start.3 = (bf16[32,1024]{1,0:T(8,128)(2,1)S(1)}, bf16[32,1024]{1,0:T(8,128)(2,1)S(1)}, u32[]{:S(2)}, u32[]{:S(2)}) collective-permute-start(bf16[32,1024]{1,0:T(8,128)(2,1)S(1)} %fusion), channel_id=1, source_target_pairs={{0,4},{1,5},{2,6},{3,7},{4,0},{5,1},{6,2},{7,3},{8,12},{9,13},{10,... | collective-permute-start | bytes 196616 | tf_op jit(solution)/shard_map/ppermute | solution.py:209
  15.1 0.7 %convert_sqrt_fusion = f32[32]{0:T(128)S(1)} fusion(s32[128]{0:T(128)} %param.13, s32[]{:T(128)S(6)} %select_n.4, s32[128]{0:T(128)} %param.14), kind=kLoop, calls=%fused_computation.8 | loop fusion | flops 64 | bytes 388 | tf_op jit(solution)/shard_map/sqrt | solution.py:283
  15.8 2.5 %collective-permute-done.3 = bf16[32,1024]{1,0:T(8,128)(2,1)S(1)} collective-permute-done((bf16[32,1024]{1,0:T(8,128)(2,1)S(1)}, bf16[32,1024]{1,0:T(8,128)(2,1)S(1)}, u32[]{:S(2)}, u32[]{:S(2)}) %collective-permute-start.3) | collective-permute-done | bytes 65568 | tf_op jit(solution)/shard_map/ppermute | solution.py:209
  18.4 0.1 divide_convert_fusion
  18.5 0.4 collective-permute-start.4
  18.9 3.9 %collective-permute-done.4 = bf16[32,1024]{1,0:T(8,128)(2,1)S(1)} collective-permute-done((bf16[32,1024]{1,0:T(8,128)(2,1)S(1)}, bf16[32,1024]{1,0:T(8,128)(2,1)S(1)}, u32[]{:S(2)}, u32[]{:S(2)}) %collective-permute-start.4) | collective-permute-done | bytes 65568 | tf_op jit(solution)/shard_map/ppermute | solution.py:209
  22.8 2.5 %collective-permute-start.7 = (bf16[64,1024]{1,0:T(8,128)(2,1)S(1)}, bf16[64,1024]{1,0:T(8,128)(2,1)S(1)}, u32[]{:S(2)}, u32[]{:S(2)}) collective-permute-start(bf16[64,1024]{1,0:T(8,128)(2,1)S(1)} %pad_maximum_fusion.own0), channel_id=1, source_target_pairs={{0,17},{1,16},{2,19},{3,18},{4,21},{5,20},{6,23},{7,22},{8,25},{9,... | collective-permute-start | bytes 393224 | tf_op jit(solution)/shard_map/ppermute | solution.py:209
  25.3 0.5 collective-permute-start.6
  25.8 0.5 collective-permute-start.5
  26.4 2.8 %copy-done = bf16[1024,3072]{1,0:T(8,128)(2,1)S(1)} copy-done((bf16[1024,3072]{1,0:T(8,128)(2,1)S(1)}, bf16[1024,3072]{1,0:T(8,128)(2,1)}, u32[]{:S(2)}) %copy-start) | copy-done | bytes 6291480
  29.1 1.2 %copy-done.2 = bf16[512,1024]{1,0:T(8,128)(2,1)S(1)} copy-done((bf16[512,1024]{1,0:T(8,128)(2,1)S(1)}, bf16[512,1024]{1,0:T(8,128)(2,1)}, u32[]{:S(2)}) %copy-start.2) | copy-done | bytes 1048600
  30.4 2.0 %local2.1 = (bf16[512,256]{1,0:T(8,128)(2,1)S(1)}, f32[512,256]{1,0:T(8,128)S(1)}, f32[512,256]{1,0:T(8,128)S(1)}) custom-call(bf16[512,1024]{1,0:T(8,128)(2,1)S(1)} %copy-done.2, bf16[1024,3072]{1,0:T(8,128)(2,1)S(1)} %copy-done), custom_call_target="tpu_custom_call" | custom-call | flops 805306368 | bytes 1572864 | tf_op jit(solution)/shard_map/local2/pallas_call | solution.py:262
  32.4 2.0 %local0.1 = (bf16[512,256]{1,0:T(8,128)(2,1)S(1)}, f32[512,256]{1,0:T(8,128)S(1)}, f32[512,256]{1,0:T(8,128)S(1)}) custom-call(bf16[512,1024]{1,0:T(8,128)(2,1)S(1)} %copy-done.2, bf16[1024,3072]{1,0:T(8,128)(2,1)S(1)} %copy-done), custom_call_target="tpu_custom_call" | custom-call | flops 805306368 | bytes 1572864 | tf_op jit(solution)/shard_map/local0/pallas_call | solution.py:262
  34.5 0.1 collective-permute-start.8
  34.6 0.5 collective-permute-start.11
  35.0 0.1 collective-permute-start.10
  35.1 0.4 collective-permute-start.9
  35.6 2.0 %local6.1 = (bf16[512,256]{1,0:T(8,128)(2,1)S(1)}, f32[512,256]{1,0:T(8,128)S(1)}, f32[512,256]{1,0:T(8,128)S(1)}) custom-call(bf16[512,1024]{1,0:T(8,128)(2,1)S(1)} %copy-done.2, bf16[1024,3072]{1,0:T(8,128)(2,1)S(1)} %copy-done), custom_call_target="tpu_custom_call" | custom-call | flops 805306368 | bytes 1572864 | tf_op jit(solution)/shard_map/local6/pallas_call | solution.py:262
  37.6 2.0 %local4.1 = (bf16[512,256]{1,0:T(8,128)(2,1)S(1)}, f32[512,256]{1,0:T(8,128)S(1)}, f32[512,256]{1,0:T(8,128)S(1)}) custom-call(bf16[512,1024]{1,0:T(8,128)(2,1)S(1)} %copy-done.2, bf16[1024,3072]{1,0:T(8,128)(2,1)S(1)} %copy-done), custom_call_target="tpu_custom_call" | custom-call | flops 805306368 | bytes 1572864 | tf_op jit(solution)/shard_map/local4/pallas_call | solution.py:262
  39.7 0.0 copy-done.3
  39.8 0.7 %copy-done.4 = bf16[1024,1024]{1,0:T(8,128)(2,1)S(1)} copy-done((bf16[1024,1024]{1,0:T(8,128)(2,1)S(1)}, bf16[1024,1024]{1,0:T(8,128)(2,1)}, u32[]{:S(2)}) %copy-start.4) | copy-done | bytes 2097176
  40.5 15.7 %final.1 = bf16[512,1024]{1,0:T(8,128)(2,1)} custom-call(s32[4]{0:T(128)S(1)} %pad_add_fusion.place, s32[2,8]{1,0:T(2,128)S(1)} %copy-done.8, bf16[64,1024]{1,0:T(8,128)(2,1)S(1)} %pad_maximum_fusion.own0, bf16[64,1024]{1,0:T(8,128)(2,1)S(1)} %collective-permute-done.5.own1, bf16[64,1024]{1,0:T(8,128)(2,1)S(1)} %collective-permute-done.6.before0.after0, ...), custom_call_target="tpu_custom_call" | custom-call | flops 3221225472 | tf_op jit(solution)/shard_map/final/pallas_call | solution.py:309
  (27 shorter events, 0.2 us)
Async XLA Ops:
  0.1 1.2 %copy-start.1 = (bf16[512,1024]{1,0:T(8,128)(2,1)S(1)}, bf16[512,1024]{1,0:T(8,128)(2,1)}, u32[]{:S(2)}) copy-start(bf16[512,1024]{1,0:T(8,128)(2,1)} %tokens.9) | copy-start | bytes 3145732
  1.3 0.7 %copy-start.6 = (s32[128]{0:T(128)S(1)}, s32[128]{0:T(128)}, u32[]{:S(2)}) copy-start(s32[128]{0:T(128)} %param.13) | copy-start | bytes 1540
  2.0 0.7 %copy-start.7 = (s32[128]{0:T(128)S(1)}, s32[128]{0:T(128)}, u32[]{:S(2)}) copy-start(s32[128]{0:T(128)} %param.14) | copy-start | bytes 1540
  3.6 5.8 %collective-permute-start = (bf16[32,1024]{1,0:T(8,128)(2,1)S(1)}, bf16[32,1024]{1,0:T(8,128)(2,1)S(1)}, u32[]{:S(2)}, u32[]{:S(2)}) collective-permute-start(bf16[32,1024]{1,0:T(8,128)(2,1)S(1)} %get-tuple-element.33), channel_id=1, source_target_pairs={{0,1},{1,0},{2,3},{3,2},{4,5},{5,4},{6,7},{7,6},{8,9},{9,8},{10,11... | collective-permute-start | bytes 196616 | tf_op jit(solution)/shard_map/ppermute | solution.py:209
  6.6 5.8 %collective-permute-start.2 = (bf16[32,1024]{1,0:T(8,128)(2,1)S(1)}, bf16[32,1024]{1,0:T(8,128)(2,1)S(1)}, u32[]{:S(2)}, u32[]{:S(2)}) collective-permute-start(bf16[32,1024]{1,0:T(8,128)(2,1)S(1)} %get-tuple-element.34), channel_id=1, source_target_pairs={{0,3},{1,2},{2,1},{3,0},{4,7},{5,6},{6,5},{7,4},{8,11},{9,10},{10,... | collective-permute-start | bytes 196616 | tf_op jit(solution)/shard_map/ppermute | solution.py:209
  8.1 4.3 %collective-permute-start.1 = (bf16[32,1024]{1,0:T(8,128)(2,1)S(1)}, bf16[32,1024]{1,0:T(8,128)(2,1)S(1)}, u32[]{:S(2)}, u32[]{:S(2)}) collective-permute-start(bf16[32,1024]{1,0:T(8,128)(2,1)S(1)} %get-tuple-element.35), channel_id=1, source_target_pairs={{0,2},{1,3},{2,0},{3,1},{4,6},{5,7},{6,4},{7,5},{8,10},{9,11},{10,... | collective-permute-start | bytes 196616 | tf_op jit(solution)/shard_map/ppermute | solution.py:209
  12.4 5.9 %collective-permute-start.3 = (bf16[32,1024]{1,0:T(8,128)(2,1)S(1)}, bf16[32,1024]{1,0:T(8,128)(2,1)S(1)}, u32[]{:S(2)}, u32[]{:S(2)}) collective-permute-start(bf16[32,1024]{1,0:T(8,128)(2,1)S(1)} %fusion), channel_id=1, source_target_pairs={{0,4},{1,5},{2,6},{3,7},{4,0},{5,1},{6,2},{7,3},{8,12},{9,13},{10,... | collective-permute-start | bytes 196616 | tf_op jit(solution)/shard_map/ppermute | solution.py:209
  18.5 4.3 %collective-permute-start.4 = (bf16[32,1024]{1,0:T(8,128)(2,1)S(1)}, bf16[32,1024]{1,0:T(8,128)(2,1)S(1)}, u32[]{:S(2)}, u32[]{:S(2)}) collective-permute-start(bf16[32,1024]{1,0:T(8,128)(2,1)S(1)} %divide_convert_fusion), channel_id=1, source_target_pairs={{0,2},{1,3},{2,0},{3,1},{4,6},{5,7},{6,4},{7,5},{8,10},{9,11},{10,... | collective-permute-start | bytes 196616 | tf_op jit(solution)/shard_map/ppermute | solution.py:209
  22.8 11.7 %collective-permute-start.7 = (bf16[64,1024]{1,0:T(8,128)(2,1)S(1)}, bf16[64,1024]{1,0:T(8,128)(2,1)S(1)}, u32[]{:S(2)}, u32[]{:S(2)}) collective-permute-start(bf16[64,1024]{1,0:T(8,128)(2,1)S(1)} %pad_maximum_fusion.own0), channel_id=1, source_target_pairs={{0,17},{1,16},{2,19},{3,18},{4,21},{5,20},{6,23},{7,22},{8,25},{9,... | collective-permute-start | bytes 393224 | tf_op jit(solution)/shard_map/ppermute | solution.py:209
  25.3 9.7 %collective-permute-start.6 = (bf16[64,1024]{1,0:T(8,128)(2,1)S(1)}, bf16[64,1024]{1,0:T(8,128)(2,1)S(1)}, u32[]{:S(2)}, u32[]{:S(2)}) collective-permute-start(bf16[64,1024]{1,0:T(8,128)(2,1)S(1)} %pad_maximum_fusion.own0), channel_id=1, source_target_pairs={{0,16},{1,17},{2,18},{3,19},{4,20},{5,21},{6,22},{7,23},{8,24},{9,... | collective-permute-start | bytes 393224 | tf_op jit(solution)/shard_map/ppermute | solution.py:209
  25.8 9.3 %collective-permute-start.5 = (bf16[64,1024]{1,0:T(8,128)(2,1)S(1)}, bf16[64,1024]{1,0:T(8,128)(2,1)S(1)}, u32[]{:S(2)}, u32[]{:S(2)}) collective-permute-start(bf16[64,1024]{1,0:T(8,128)(2,1)S(1)} %pad_maximum_fusion.own0), channel_id=1, source_target_pairs={{0,1},{1,0},{2,3},{3,2},{4,5},{5,4},{6,7},{7,6},{8,9},{9,8},{10,11... | collective-permute-start | bytes 393224 | tf_op jit(solution)/shard_map/ppermute | solution.py:209
  26.4 2.8 %copy-start = (bf16[1024,3072]{1,0:T(8,128)(2,1)S(1)}, bf16[1024,3072]{1,0:T(8,128)(2,1)}, u32[]{:S(2)}) copy-start(bf16[1024,3072]{1,0:T(8,128)(2,1)} %w_qkv.9) | copy-start | bytes 18874372
  29.1 1.2 %copy-start.2 = (bf16[512,1024]{1,0:T(8,128)(2,1)S(1)}, bf16[512,1024]{1,0:T(8,128)(2,1)}, u32[]{:S(2)}) copy-start(bf16[512,1024]{1,0:T(8,128)(2,1)} %tokens.9) | copy-start | bytes 3145732
  32.4 7.3 %slice-start = ((s8[6291456]{0:T(1024)(128)(4,1)}), s8[4194304]{0:T(1024)(128)(4,1)S(1)}, s32[]{:S(2)}) async-start(s8[6291456]{0:T(1024)(128)(4,1)} %bitcast.12), calls=%async_computation | async-start | bytes 8388608
  34.5 5.3 %slice-start.1 = ((s8[6291456]{0:T(1024)(128)(4,1)}), s8[2097152]{0:T(1024)(128)(4,1)S(1)}, s32[]{:S(2)}) async-start(s8[6291456]{0:T(1024)(128)(4,1)} %bitcast.12), calls=%async_computation.1 | async-start | bytes 4194304
  34.5 5.2 %collective-permute-start.8 = (bf16[64,1024]{1,0:T(8,128)(2,1)S(1)}, bf16[64,1024]{1,0:T(8,128)(2,1)S(1)}, u32[]{:S(2)}, u32[]{:S(2)}) collective-permute-start(bf16[64,1024]{1,0:T(8,128)(2,1)S(1)} %pad_maximum_fusion.own0), channel_id=1, source_target_pairs={{0,8},{1,9},{2,10},{3,11},{4,12},{5,13},{6,14},{7,15},{8,0},{9,1},... | collective-permute-start | bytes 393224 | tf_op jit(solution)/shard_map/ppermute | solution.py:209
  34.6 5.1 %collective-permute-start.11 = (bf16[64,1024]{1,0:T(8,128)(2,1)S(1)}, bf16[64,1024]{1,0:T(8,128)(2,1)S(1)}, u32[]{:S(2)}, u32[]{:S(2)}) collective-permute-start(bf16[64,1024]{1,0:T(8,128)(2,1)S(1)} %collective-permute-done.7.before1.after1), channel_id=1, source_target_pairs={{0,8},{1,9},{2,10},{3,11},{4,12},{5,13},{6,14},{7,15},{8,0},{9,1},... | collective-permute-start | bytes 393224 | tf_op jit(solution)/shard_map/ppermute | solution.py:209
  35.0 4.6 %collective-permute-start.10 = (bf16[64,1024]{1,0:T(8,128)(2,1)S(1)}, bf16[64,1024]{1,0:T(8,128)(2,1)S(1)}, u32[]{:S(2)}, u32[]{:S(2)}) collective-permute-start(bf16[64,1024]{1,0:T(8,128)(2,1)S(1)} %collective-permute-done.6.before0.after0), channel_id=1, source_target_pairs={{0,8},{1,9},{2,10},{3,11},{4,12},{5,13},{6,14},{7,15},{8,0},{9,1},... | collective-permute-start | bytes 393224 | tf_op jit(solution)/shard_map/ppermute | solution.py:209
  35.1 4.6 %collective-permute-start.9 = (bf16[64,1024]{1,0:T(8,128)(2,1)S(1)}, bf16[64,1024]{1,0:T(8,128)(2,1)S(1)}, u32[]{:S(2)}, u32[]{:S(2)}) collective-permute-start(bf16[64,1024]{1,0:T(8,128)(2,1)S(1)} %collective-permute-done.5.own1), channel_id=1, source_target_pairs={{0,8},{1,9},{2,10},{3,11},{4,12},{5,13},{6,14},{7,15},{8,0},{9,1},... | collective-permute-start | bytes 393224 | tf_op jit(solution)/shard_map/ppermute | solution.py:209
  35.6 4.2 %copy-start.5 = (bf16[1024,1024]{1,0:T(8,128)(2,1)S(1)}, bf16[1024,1024]{1,0:T(8,128)(2,1)}, u32[]{:S(2)}) copy-start(bf16[1024,1024]{1,0:T(8,128)(2,1)} %w_out.1) | copy-start | bytes 6291460
  37.6 2.2 %copy-start.3 = (bf16[1024,2048]{1,0:T(8,128)(2,1)S(1)}, bf16[1024,2048]{1,0:T(8,128)(2,1)}, u32[]{:S(2)}) copy-start(bf16[1024,2048]{1,0:T(8,128)(2,1)} %w_kv2.1) | copy-start | bytes 12582916
  37.6 2.9 %copy-start.4 = (bf16[1024,1024]{1,0:T(8,128)(2,1)S(1)}, bf16[1024,1024]{1,0:T(8,128)(2,1)}, u32[]{:S(2)}) copy-start(bf16[1024,1024]{1,0:T(8,128)(2,1)} %w_co.1) | copy-start | bytes 6291460
  37.6 2.9 %copy-start.8 = (s32[2,8]{1,0:T(2,128)S(1)}, s32[2,8]{1,0:T(2,128)}, u32[]{:S(2)}) copy-start(s32[2,8]{1,0:T(2,128)} %lists.1) | copy-start | bytes 196

commit v2 on v1

v2 whole, which is shorter than its diff:
```python
import functools
import math

import jax
import jax.numpy as jnp
from jax import lax
from jax.experimental import pallas as pl
from jax.experimental.pallas import tpu as pltpu
from jax.sharding import PartitionSpec as P

HEADS = 8
KB = 16
QB = 256
BLK = 128
MIB = 1 << 20
AXES = ("coarse", "fine")
F32 = jnp.float32
BF16 = jnp.bfloat16

VM = pl.BlockSpec(memory_space=pltpu.VMEM)
SM = pl.BlockSpec(memory_space=pltpu.SMEM)
ANY = pl.BlockSpec(memory_space=pl.ANY)
FAR = pl.BlockSpec(memory_space=pltpu.HBM)


def cdiv(a, b):
    return -(-a // b)


def dot(a, b):
    return jnp.dot(a, b, preferred_element_type=F32)


def dot_t(a, b):
    return lax.dot_general(a, b, (((1,), (1,)), ((), ())), preferred_element_type=F32)


def call(kernel, outs, in_specs, scratch, limit, flops, moved, name, out_specs=None):
    return pl.pallas_call(
        kernel,
        out_shape=outs,
        in_specs=in_specs,
        out_specs=out_specs or jax.tree.map(lambda _: VM, outs),
        scratch_shapes=scratch,
        compiler_params=pltpu.CompilerParams(vmem_limit_bytes=limit * MIB),
        cost_estimate=pl.CostEstimate(flops=flops, bytes_accessed=moved, transcendentals=0),
        name=name,
    )


def sums_kernel(chunk, place, starts_far, ends_far, tokens_far, own, send, tokens, roots, acc, root, starts, ends, sem):
    copies = [
        pltpu.make_async_copy(source, target, sem.at[i])
        for i, (source, target) in enumerate(((starts_far, starts), (ends_far, ends), (tokens_far, tokens)))
    ]
    for copy in copies:
        copy.start()
    rows = tokens.shape[0]
    owned = starts.shape[1]
    mine = place[0]
    where_ = place[1] + lax.broadcasted_iota(jnp.int32, (BLK, rows), 1)
    copies[0].wait()
    copies[1].wait()
    members = []
    for s in range(owned // BLK):
        at = slice(s * BLK, (s + 1) * BLK)
        low = jnp.broadcast_to(starts[:, at], (BLK, BLK)).T
        high = jnp.broadcast_to(ends[:, at], (BLK, BLK)).T
        root[at, :] = jnp.sqrt((high - low).astype(F32))
        low = jnp.concatenate([low] * (rows // BLK), axis=1)
        high = jnp.concatenate([high] * (rows // BLK), axis=1)
        members.append(jnp.where((where_ >= low) & (where_ < high), 1.0, 0.0).astype(BF16))
    copies[2].wait()
    for s in range(owned // BLK):
        acc[s * BLK : (s + 1) * BLK, :] = dot(members[s], tokens[...])
    own[...] = acc[pl.ds(pl.multiple_of(mine * chunk, chunk), chunk), :]
    for i, r in enumerate((0, 2)):
        roots[i * chunk : (i + 1) * chunk, :] = root[pl.ds(pl.multiple_of((mine ^ r) * chunk, chunk), chunk), :]
    for r in range(1, 4):
        theirs = pl.multiple_of((mine ^ r) * chunk, chunk)
        send[r - 1][...] = acc[pl.ds(theirs, chunk), :].astype(BF16)


def add_kernel(own, *rest):
    *got, total, half = rest
    sums = own[...]
    for cells in got:
        sums = sums + cells[...].astype(F32)
    total[...] = sums
    half[...] = sums.astype(BF16)


def pool_kernel(total, across, beside, corner, roots, pooled):
    chunk, width = total.shape
    mine = total[...] + across[...].astype(F32)
    theirs = beside[...].astype(F32) + corner[...].astype(F32)
    root = jnp.concatenate([roots[...]] * (width // BLK), axis=1)
    pooled[:chunk, :] = (mine / root[:chunk]).astype(BF16)
    pooled[chunk:, :] = (theirs / root[chunk:]).astype(BF16)


def local_kernel(first, heads, size, scale, tokens, weights, after, query, mix, level):
    del after
    width = tokens.shape[1]
    span = heads * size
    parts = [
        dot(tokens[...], weights[:, k * width + first * size : k * width + first * size + span]).astype(BF16)
        for k in range(3)
    ]
    attend_here(heads, size, scale, parts, query, mix, level)


def far_kernel(first, heads, size, scale, tokens, w_far, after, query, mix, level, weights, sem):
    del after
    width = tokens.shape[1]
    span = heads * size
    copies = []
    for k in range(3):
        at = k * width + first * size
        copies.append(pltpu.make_async_copy(w_far.at[:, at : at + span], weights.at[k], sem.at[k]))
        copies[k].start()
    parts = []
    for k in range(3):
        copies[k].wait()
        parts.append(dot(tokens[...], weights[k]).astype(BF16))
    attend_here(heads, size, scale, parts, query, mix, level)


def attend_here(heads, size, scale, parts, query, mix, level):
    queries, keys, cells = parts
    query[...] = queries
    ones = jnp.ones((keys.shape[0], size), BF16)
    for i in range(heads):
        at = slice(i * size, (i + 1) * size)
        scores = dot_t(queries[:, at], keys[:, at])
        highest = jnp.max(scores, axis=1, keepdims=True)
        expos = jnp.exp2((scores - highest) * scale).astype(BF16)
        both = dot(expos, jnp.concatenate([cells[:, at], ones], axis=1))
        total = both[:, size:]
        mix[:, at] = both[:, :size] / total
        level[:, at] = highest * scale + jnp.log2(total)


def normalize(cells):
    return cells * lax.rsqrt(jnp.mean(cells * cells, axis=1, keepdims=True) + 1e-06)


def rows_kernel(cells, w_qkv, out):
    for c in range(0, out.shape[1], 512):
        out[:, c : c + 512] = dot(cells[...], w_qkv[:, c : c + 512]).astype(BF16)


def move(chunk, cells, targets):
    for i, (target, to, columns) in enumerate(targets):
        target[pl.ds(pl.multiple_of(to, chunk), chunk), columns] = cells[i * chunk : (i + 1) * chunk, :]


def near_kernel(chunk, place, own1, ends0, ends1, done, w_qkv, pairs):
    width = w_qkv.shape[0]
    owned = chunk * 4
    mine = place[0]
    cells = jnp.concatenate([own1[...], ends0[...], ends1[...]], axis=0)
    at = [(mine ^ r) * chunk for r in (1, 3)]
    at += [owned + (mine ^ r ^ 2) * chunk for r in (0, 2, 1, 3)]
    for c in range(0, 2 * width, 512):
        columns = slice(c, c + 512)
        found = dot(cells, w_qkv[:, width + c : width + c + 512]).astype(BF16)
        move(chunk, found, [(pairs, to, columns) for to in at])
    before = [mine * chunk, (mine ^ 2) * chunk]
    move(chunk, done[:, width:], [(pairs, to, slice(None)) for to in before])


def final_kernel(
    chunk, reach, size, scale, total_rows, head_groups,
    place, lists, own1, pair0, pair1, side0, side1, done, near_pairs,
    w_qkv, w_co, w_kv2, w_out, *rest,
):
    parts = len(rest) - 8
    held = [(p, i) for p, count in enumerate(head_groups) for i in range(count)]
    query, mix, level = (rest[k:parts:3] for k in range(3))
    out, far_pairs, coarse_query, state, listed, attended, ready, sem = rest[parts:]
    width = state.shape[1]
    owned = chunk * 4
    mine = place[0]
    core = place[2]
    owner = place[3]

    own_at = [owned + (mine ^ r) * chunk for r in (0, 2, 1, 3)]
    pair_at = [(1 - core) * owned + (mine ^ r) * chunk for r in (0, 2, 1, 3)]
    side_at = [core * owned + (mine ^ r) * chunk for r in (0, 2, 1, 3)]
    pair_to = [(1 - core) * 2 * owned + (mine ^ r) * chunk for r in (0, 2, 1, 3)]
    side_to = [core * 2 * owned + (mine ^ r) * chunk for r in (0, 2, 1, 3)]
    rows = jnp.concatenate([pair0[...], pair1[...], side0[...], side1[...], own1[...]], axis=0)
    for c in range(0, width, 512):
        found = dot(rows, w_qkv[:, c : c + 512]).astype(BF16)
        move(chunk, found, [(coarse_query, to, slice(c, c + 512)) for to in pair_to + side_to + own_at[2:]])
    rows = rows[: 8 * chunk]
    for c in range(0, 2 * width, 512):
        found = dot(rows, w_qkv[:, width + c : width + c + 512]).astype(BF16)
        move(chunk, found, [(far_pairs, to, slice(c, c + 512)) for to in pair_at + side_at])
    move(chunk, done[:, :width], [(coarse_query, to, slice(None)) for to in own_at[:2]])

    runs = (
        (near_pairs, owned, reach),
        (far_pairs, 0, owned),
        (near_pairs, 0, owned),
        (far_pairs, owned, owned),
        (near_pairs, owned + reach, reach),
    )

    def window(first, count, columns):
        cells = []
        start = 0
        for source, at, rows in runs:
            low, high = max(first, start), min(first + count, start + rows)
            if low < high:
                cells.append(source[at + low - start : at + high - start, columns])
            start += rows
        return jnp.concatenate(cells, axis=0)

    span = BLK + 2 * reach
    row = lax.broadcasted_iota(jnp.int32, (BLK, span), 0)
    column = lax.broadcasted_iota(jnp.int32, (BLK, span), 1)
    inside = (column >= row) & (column <= row + 2 * reach)
    ones = jnp.ones((span, size), BF16)
    for first in range(0, 3 * owned, BLK):
        heads = [slice(h * size, (h + 1) * size) for h in range(HEADS)]
        scores = []
        for at in heads:
            score = dot_t(coarse_query[first : first + BLK, at], window(first, span, at))
            scores.append(jnp.where(inside, score, -1e30))
        tops = [jnp.max(score, axis=1, keepdims=True) for score in scores]
        expos = [jnp.exp2((score - top) * scale).astype(BF16) for score, top in zip(scores, tops)]
        mixed = []
        for at, expo in zip(heads, expos):
            cells = window(first, span, slice(width + at.start, width + at.stop))
            both = dot(expo, jnp.concatenate([cells, ones], axis=1))
            mixed.append((both[:, :size] / both[:, size:]).astype(BF16))
        context = dot(jnp.concatenate(mixed, axis=1), w_co[...])
        state[first : first + BLK, :] = normalize(context).astype(BF16)

    base = (owner - 1) * owned
    groups, picks = lists.shape
    for n in range(groups):
        for m in range(picks):
            at = lax.rem(lists[n, m] * KB - base + total_rows, total_rows)
            to = (n * picks + m) * KB
            listed[to : to + KB, :] = state[pl.ds(pl.multiple_of(at, KB), KB), :]
    here = picks * KB
    ones_here = jnp.ones((here, size), BF16)
    span2 = 2 * size
    second = [
        [dot(listed[...], w_kv2[:, k * width + c : k * width + c + span2]).astype(BF16) for k in range(2)]
        for c in range(0, width, span2)
    ]

    def fine(units):
        kept = []
        for n, h in units:
            part, place_in = held[h]
            at = slice(place_in * size, (place_in + 1) * size)
            keys, cells = (c[n * here : (n + 1) * here, h % 2 * size : (h % 2 + 1) * size] for c in second[h // 2])
            rows = slice(n * QB, (n + 1) * QB)
            kept.append((part, rows, at, cells, dot_t(query[part][rows, at], keys) * scale))
        tops = [
            jnp.maximum(level[part][rows, at], jnp.max(scores, axis=1, keepdims=True))
            for part, rows, at, cells, scores in kept
        ]
        boths = []
        for (part, rows, at, cells, scores), top in zip(kept, tops):
            expos = jnp.exp2(scores - top[:, :here]).astype(BF16)
            boths.append(dot(expos, jnp.concatenate([cells, ones_here], axis=1)))
        for (n, h), (part, rows, at, cells, scores), top, both in zip(units, kept, tops, boths):
            keep = jnp.exp2(level[part][rows, at] - top)
            mixed = mix[part][rows, at] * keep + both[:, :size]
            attended[rows, h * size : (h + 1) * size] = (mixed / (keep + both[:, size:])).astype(BF16)

    units = [(n, h) for h in range(HEADS) for n in range(groups)]
    for u in range(0, len(units), 8):
        fine(units[u : u + 8])
    copies = []
    for first in range(0, out.shape[0], BLK):
        some = slice(first, first + BLK)
        ready[some, :] = normalize(dot(attended[some, :], w_out[...])).astype(BF16)
        copies.append(pltpu.make_async_copy(ready.at[some], out.at[some], sem.at[len(copies)]))
        copies[-1].start()
    for copy in copies:
        copy.wait()


def swap(cells, coarse_bit, fine_bit):
    coarse_count = lax.axis_size("coarse")
    fine_count = lax.axis_size("fine")
    pairs = [
        (c * fine_count + f, (c ^ coarse_bit) * fine_count + (f ^ fine_bit))
        for c in range(coarse_count)
        for f in range(fine_count)
    ]
    return lax.ppermute(cells, AXES, pairs)


def shift(cells, chips, fine_bit):
    coarse_count = lax.axis_size("coarse")
    fine_count = lax.axis_size("fine")
    pairs = [
        (c * fine_count + f, ((c + 2 * chips) % coarse_count) * fine_count + (f ^ fine_bit))
        for c in range(coarse_count)
        for f in range(fine_count)
    ]
    return lax.ppermute(cells, AXES, pairs)


def body(tokens, w_qkv, w_coarse_out, w_kv2, w_out, seg_start, seg_end, block_lists):
    rows_here, width = tokens.shape
    size = width // HEADS
    fine_count = lax.axis_size("fine")
    coarse_count = lax.axis_size("coarse")
    fine_index = lax.axis_index("fine")
    coarse_index = lax.axis_index("coarse")
    owned = seg_start.shape[0]
    chunk = owned // 4
    reach = owned // 2
    scale = math.log2(math.e) / math.sqrt(size)
    mine = fine_index & 3
    big = coarse_count > 4
    far = functools.partial(pltpu.with_memory_space_constraint, memory_space=pltpu.HBM)
    kept = jax.ShapeDtypeStruct if big else pltpu.VMEM
    near = (lambda c: c) if big else functools.partial(pltpu.with_memory_space_constraint, memory_space=pltpu.VMEM)
    first_row = coarse_index * (rows_here * fine_count) + fine_index * rows_here
    place = jnp.stack([mine, first_row, coarse_index & 1, coarse_index]).astype(jnp.int32)

    own, *send, tokens, roots = call(
        lambda *refs: sums_kernel(chunk, *refs[:4], refs[4], refs[5:8], *refs[8:]),
        (
            jax.ShapeDtypeStruct((chunk, width), F32),
            *[jax.ShapeDtypeStruct((chunk, width), BF16)] * 3,
            kept(tokens.shape, BF16),
            jax.ShapeDtypeStruct((2 * chunk, BLK), F32),
        ),
        [SM, FAR, FAR, FAR],
        [
            pltpu.VMEM((owned, width), F32),
            pltpu.VMEM((owned, BLK), F32),
            pltpu.VMEM((1, owned), jnp.int32),
            pltpu.VMEM((1, owned), jnp.int32),
            pltpu.SemaphoreType.DMA((3,)),
        ],
        24 if big else 8,
        2 * owned * rows_here * width,
        rows_here * width * 2,
        "sums",
    )(place, far(seg_start.reshape(1, owned)), far(seg_end.reshape(1, owned)), far(tokens))

    head_groups = (2, 2, 4)

    def local(first, heads, weights, after):
        span = heads * size
        results = (
            jax.ShapeDtypeStruct((rows_here, span), BF16),
            jax.ShapeDtypeStruct((rows_here, span), F32),
            jax.ShapeDtypeStruct((rows_here, span), F32),
        )
        cost = 2 * rows_here * width * 3 * span, 0, f"local{first}"
        if first + heads < HEADS:
            return call(
                functools.partial(far_kernel, first, heads, size, scale),
                results,
                [VM, FAR, ANY],
                [pltpu.VMEM((3, width, span), BF16), pltpu.SemaphoreType.DMA((3,))],
                24 if big else 10,
                *cost,
            )(tokens, far(weights), after)
        kernel = functools.partial(local_kernel, first, heads, size, scale)
        return call(kernel, results, [VM, VM, ANY], [], 24 if big else 10, *cost)(tokens, weights, after)

    def beside(value, made):
        value, first = lax.optimization_barrier((value, made[0]))
        return value, [first, *made[1:]]

    got = [swap(send[r - 1], 0, r) for r in range(1, 4)]
    own, part = beside(own, local(0, 2, w_qkv, send[0]))
    parts = list(part)
    rows32 = jax.ShapeDtypeStruct((chunk, width), F32)
    rows16 = jax.ShapeDtypeStruct((chunk, width), BF16)

    def add(total, got):
        return call(
            add_kernel, (rows32, rows16), [VM] * (1 + len(got)), [], 8 if big else 4, 0, chunk * width, "add"
        )(total, *got)

    sums, half = add(own, got)
    bit = 8
    while bit < fine_count:
        sums, half = add(sums, [swap(half, 0, bit)])
        bit *= 2
    across, beside_half, corner = (swap(half, 0, bit) for bit in (4, 2, 6))
    sums, part = beside(sums, local(2, 2, w_qkv, half))
    parts.extend(part)
    own0 = call(
        pool_kernel,
        jax.ShapeDtypeStruct((2 * chunk, width), BF16),
        [VM] * 5,
        [],
        8 if big else 4,
        0,
        chunk * width,
        "pool",
    )(sums, across, beside_half, corner, roots)
    own1 = swap(own0, 0, 1)
    chips = coarse_count // 2
    core = coarse_index & 1
    if chips == 2:
        ends0 = side0 = swap(own0, 2, 0)
        ends1 = side1 = swap(own0, 2, 1)
    else:
        before0, before1 = shift(own0, 1, 0), shift(own0, 1, 1)
        after0, after1 = shift(own0, -1, 0), shift(own0, -1, 1)
        side0 = jnp.where(core == 0, after0, before0)
        side1 = jnp.where(core == 0, after1, before1)
        upper = jnp.repeat(jnp.stack([mine >= 2, mine < 2]), chunk)[:, None]
        ends0 = jnp.where(upper, before0, after0)
        ends1 = jnp.where(upper, before1, after1)
    done = call(
        rows_kernel,
        jax.ShapeDtypeStruct((2 * chunk, 3 * width), BF16),
        [VM, VM],
        [],
        40 if big else 8,
        2 * 2 * chunk * width * 3 * width,
        0,
        "rows",
    )(own0, w_qkv)
    side0, part = beside(side0, local(4, 4, w_qkv, own0))
    side0, (done,) = beside(side0, [done])
    own0 = lax.optimization_barrier((own0, side0))[0]
    parts.extend(part)
    pair0, pair1, side0, side1 = (swap(c, 1, 0) for c in (own0, own1, side0, side1))
    near_pairs = call(
        functools.partial(near_kernel, chunk),
        jax.ShapeDtypeStruct((2 * owned, 2 * width), BF16),
        [SM] + [VM] * 5,
        [],
        40 if big else 8,
        2 * owned * width * 3 * width,
        0,
        "near",
    )(place, own1, ends0, ends1, done, w_qkv)

    listed_rows = block_lists.shape[0] * block_lists.shape[1] * KB
    return call(
        functools.partial(final_kernel, chunk, reach, size, scale, owned * coarse_count, head_groups),
        jax.ShapeDtypeStruct((rows_here, width), BF16),
        [SM, SM] + [VM] * (11 + len(parts)),
        [
            pltpu.VMEM((2 * owned, 2 * width), BF16),
            pltpu.VMEM((3 * owned, width), BF16),
            pltpu.VMEM((3 * owned, width), BF16),
            pltpu.VMEM((listed_rows, width), BF16),
            pltpu.VMEM((rows_here, width), BF16),
            pltpu.VMEM((rows_here, width), BF16),
            pltpu.SemaphoreType.DMA((rows_here // BLK,)),
        ],
        60 if big else 14,
        2 * 2 * owned * width * 3 * width,
        0,
        "final",
        FAR,
    )(
        place, block_lists, own1, pair0, pair1, side0, side1, done, near_pairs,
        w_qkv, near(w_coarse_out), near(w_kv2), near(w_out), *parts,
    )


def solution(mesh):
    placed = (
        P(("coarse", "fine"), None),
        P(),
        P(),
        P(),
        P(),
        P("coarse"),
        P("coarse"),
        P(("coarse", "fine"), None),
    )
    return jax.shard_map(
        body, mesh=mesh, in_specs=placed, out_specs=P(("coarse", "fine"), None), check_vma=False
    )
```

time: 56.4 us -> 41.6 us (0.74)
  waiting for transfers between devices: 10.7 us -> 0.92 us
  local copies, waits for them, and re-layouts: 7.32 us -> 0.11 us
  Pallas kernels: 24.7 us -> 26.2 us
  starting transfers between devices: 12.3 us -> 13.7 us
  other arithmetic: 0.95 us -> 0.08 us
    ppermute x12 -> x13, waiting for transfers between devices: 10.7 us -> 0.92 us  [swap(): return lax.ppermute(cells, AXES, pairs)]
    pallas_call x5 -> x8, Pallas kernels: 9.04 us -> 16.3 us  [the longest x2 7.85 us: local(): call(functools.partial(far_kernel, first, heads, size, scale), results, [...]
    unnamed x22 -> x12, local copies, waits for them, and re-layouts: 7.31 us -> 0.11 us
    pallas_call x1, Pallas kernels: 15.7 us -> 9.93 us  [body(): call(functools.partial(final_kernel, chunk, reach, size, scale, owned * c...]
    ppermute x12 -> x13, starting transfers between devices: 12.3 us -> 13.7 us  [swap(): return lax.ppermute(cells, AXES, pairs)]
    sqrt x1 -> x0, other arithmetic: 0.75 us -> none  [body(): roots = jnp.sqrt(spans)[:, None]]
  transfers between devices with their start and end apart: 12 -> 13, of which waited for: 4 -> 2; matrix products, arithmetic and copies ran while one was open for 1% -> 0% of each run, Pallas kernels for 14% -> 34%
where the time goes in v2:
time: 41.6 us; the launch traced here: 41.4 us
  Pallas kernels  26.2 us (63%)
  starting transfers between devices  13.7 us (33%)
  waiting for transfers between devices  0.92 us (2%)
    ppermute x13, starting transfers between devices, swap(): return lax.ppermute(cells, AXES, pairs)  13.7 us
    pallas_call x1, Pallas kernels, body(): call(functools.partial(final_kernel, chunk, reach, size, scale, owned * c...  9.93 us
    pallas_call x2, Pallas kernels, local(): call(functools.partial(far_kernel, first, heads, size, scale), results, [...  7.85 us
    pallas_call x1, Pallas kernels, local(): call(kernel, results, [VM, VM, ANY], [], 24 if big else 10, *cost)  3.4 us
    pallas_call x1, Pallas kernels, body(): call(lambda *refs: sums_kernel(chunk, *refs[:4], refs[4], refs[5:8], *ref...  2.16 us
    pallas_call x1, Pallas kernels, body(): call(functools.partial(near_kernel, chunk), jax.ShapeDtypeStruct((2 * own...  1.58 us
    pallas_call x1, Pallas kernels, body(): call(rows_kernel, jax.ShapeDtypeStruct((2 * chunk, 3 * width), BF16), [VM...  1.22 us
    ppermute x13, waiting for transfers between devices, swap(): return lax.ppermute(cells, AXES, pairs)  0.92 us
  transfers between devices with their start and end apart: 13, of which 2 were waited for; matrix products, arithmetic and copies ran while one was open for 0% of the time, Pallas kernels for 34%

profile of v2, /device:TPU:0, one launch (start us, length us, event | category | flops | bytes accessed | tf_op | source)
XLA Modules:
  0.0 41.4 jit_solution(3139841387067643657)
XLA Ops:
  0.0 0.1 pad_add_fusion.refs_0_.place
  0.1 2.2 %sums.1 = (f32[32,1024]{1,0:T(8,128)S(1)}, bf16[32,1024]{1,0:T(8,128)(2,1)S(1)}, bf16[32,1024]{1,0:T(8,128)(2,1)S(1)}, bf16[32,1024]{1,0:T(8,128)(2,1)S(1)}, bf1...) custom-call(s32[4]{0:T(128)S(1)} %pad_add_fusion.refs_0_.place, s32[1,128]{1,0:T(1,128)} %bitcast.8, s32[1,128]{1,0:T(1,128)} %bitcast.9, ...), custom_call_target="tpu_custom_call" | custom-call | flops 134217728 | bytes 1048576 | tf_op jit(solution)/shard_map/sums/pallas_call | solution.py:332
  2.2 3.1 %collective-permute-start.1 = (bf16[32,1024]{1,0:T(8,128)(2,1)S(1)}, bf16[32,1024]{1,0:T(8,128)(2,1)S(1)}, u32[]{:S(2)}, u32[]{:S(2)}) collective-permute-start(bf16[32,1024]{1,0:T(8,128)(2,1)S(1)} %get-tuple-element.36), channel_id=1, source_target_pairs={{0,2},{1,3},{2,0},{3,1},{4,6},{5,7},{6,4},{7,5},{8,10},{9,11},{10,... | collective-permute-start | bytes 196616 | tf_op jit(solution)/shard_map/ppermute | solution.py:299
  5.3 1.4 %collective-permute-start.2 = (bf16[32,1024]{1,0:T(8,128)(2,1)S(1)}, bf16[32,1024]{1,0:T(8,128)(2,1)S(1)}, u32[]{:S(2)}, u32[]{:S(2)}) collective-permute-start(bf16[32,1024]{1,0:T(8,128)(2,1)S(1)} %get-tuple-element.37), channel_id=1, source_target_pairs={{0,3},{1,2},{2,1},{3,0},{4,7},{5,6},{6,5},{7,4},{8,11},{9,10},{10,... | collective-permute-start | bytes 196616 | tf_op jit(solution)/shard_map/ppermute | solution.py:299
  6.7 0.1 collective-permute-start
  6.9 4.0 %local0.1 = (bf16[512,256]{1,0:T(8,128)(2,1)S(1)}, f32[512,256]{1,0:T(8,128)S(1)}, f32[512,256]{1,0:T(8,128)S(1)}) custom-call(bf16[512,1024]{1,0:T(8,128)(2,1)S(1)} %get-tuple-element.32.tokens, bf16[1024,3072]{1,0:T(8,128)(2,1)} %w_qkv.5, bf16[32,1024]{1,0:T(8,128)(2,1)S(1)} %get-tuple-element.33.after), custom_call_target="tpu_custom_call" | custom-call | flops 805306368 | tf_op jit(solution)/shard_map/local0/pallas_call | solution.py:365
  10.9 0.0 collective-permute-done.1.rest_1_
  10.9 0.0 collective-permute-done.2.rest_2_
  10.9 0.4 collective-permute-done.rest_0_
  11.3 0.0 slice-start.1
  11.4 3.7 %collective-permute-start.5 = (bf16[32,1024]{1,0:T(8,128)(2,1)S(1)}, bf16[32,1024]{1,0:T(8,128)(2,1)S(1)}, u32[]{:S(2)}, u32[]{:S(2)}) collective-permute-start(bf16[32,1024]{1,0:T(8,128)(2,1)S(1)} %get-tuple-element.39.after), channel_id=1, source_target_pairs={{0,6},{1,7},{2,4},{3,5},{4,2},{5,3},{6,0},{7,1},{8,14},{9,15},{10,... | collective-permute-start | bytes 196616 | tf_op jit(solution)/shard_map/ppermute | solution.py:299
  15.0 0.8 %collective-permute-start.3 = (bf16[32,1024]{1,0:T(8,128)(2,1)S(1)}, bf16[32,1024]{1,0:T(8,128)(2,1)S(1)}, u32[]{:S(2)}, u32[]{:S(2)}) collective-permute-start(bf16[32,1024]{1,0:T(8,128)(2,1)S(1)} %get-tuple-element.39.after), channel_id=1, source_target_pairs={{0,4},{1,5},{2,6},{3,7},{4,0},{5,1},{6,2},{7,3},{8,12},{9,13},{10,... | collective-permute-start | bytes 196616 | tf_op jit(solution)/shard_map/ppermute | solution.py:299
  15.8 3.9 %local2.1 = (bf16[512,256]{1,0:T(8,128)(2,1)S(1)}, f32[512,256]{1,0:T(8,128)S(1)}, f32[512,256]{1,0:T(8,128)S(1)}) custom-call(bf16[512,1024]{1,0:T(8,128)(2,1)S(1)} %get-tuple-element.32.tokens, bf16[1024,3072]{1,0:T(8,128)(2,1)} %w_qkv.5, bf16[32,1024]{1,0:T(8,128)(2,1)S(1)} %get-tuple-element.39.after), custom_call_target="tpu_custom_call" | custom-call | flops 805306368 | tf_op jit(solution)/shard_map/local2/pallas_call | solution.py:365
  19.7 0.5 %collective-permute-done.3.across = bf16[32,1024]{1,0:T(8,128)(2,1)S(1)} collective-permute-done((bf16[32,1024]{1,0:T(8,128)(2,1)S(1)}, bf16[32,1024]{1,0:T(8,128)(2,1)S(1)}, u32[]{:S(2)}, u32[]{:S(2)}) %collective-permute-start.3) | collective-permute-done | bytes 65568 | tf_op jit(solution)/shard_map/ppermute | solution.py:299
  20.2 2.5 %collective-permute-start.11 = (bf16[64,1024]{1,0:T(8,128)(2,1)S(1)}, bf16[64,1024]{1,0:T(8,128)(2,1)S(1)}, u32[]{:S(2)}, u32[]{:S(2)}) collective-permute-start(bf16[64,1024]{1,0:T(8,128)(2,1)S(1)} %pool.1.after.cells), channel_id=1, source_target_pairs={{0,17},{1,16},{2,19},{3,18},{4,21},{5,20},{6,23},{7,22},{8,25},{9,... | collective-permute-start | bytes 393224 | tf_op jit(solution)/shard_map/ppermute | solution.py:299
  22.7 0.5 %collective-permute-start.7 = (bf16[64,1024]{1,0:T(8,128)(2,1)S(1)}, bf16[64,1024]{1,0:T(8,128)(2,1)S(1)}, u32[]{:S(2)}, u32[]{:S(2)}) collective-permute-start(bf16[64,1024]{1,0:T(8,128)(2,1)S(1)} %pool.1.after.cells), channel_id=1, source_target_pairs={{0,16},{1,17},{2,18},{3,19},{4,20},{5,21},{6,22},{7,23},{8,24},{9,... | collective-permute-start | bytes 393224 | tf_op jit(solution)/shard_map/ppermute | solution.py:299
  23.3 0.5 %collective-permute-start.6 = (bf16[64,1024]{1,0:T(8,128)(2,1)S(1)}, bf16[64,1024]{1,0:T(8,128)(2,1)S(1)}, u32[]{:S(2)}, u32[]{:S(2)}) collective-permute-start(bf16[64,1024]{1,0:T(8,128)(2,1)S(1)} %pool.1.after.cells), channel_id=1, source_target_pairs={{0,1},{1,0},{2,3},{3,2},{4,5},{5,4},{6,7},{7,6},{8,9},{9,8},{10,11... | collective-permute-start | bytes 393224 | tf_op jit(solution)/shard_map/ppermute | solution.py:299
  23.8 1.2 %rows.1.done = bf16[64,3072]{1,0:T(8,128)(2,1)S(1)} custom-call(bf16[64,1024]{1,0:T(8,128)(2,1)S(1)} %pool.1.after.cells, bf16[1024,3072]{1,0:T(8,128)(2,1)S(1)} %bitcast.7), custom_call_target="tpu_custom_call" | custom-call | flops 402653184 | tf_op jit(solution)/shard_map/rows/pallas_call | solution.py:423
  25.0 0.0 copy-start.2
  25.0 3.4 %local4.1 = (bf16[512,512]{1,0:T(8,128)(2,1)S(1)}, f32[512,512]{1,0:T(8,128)S(1)}, f32[512,512]{1,0:T(8,128)S(1)}) custom-call(bf16[512,1024]{1,0:T(8,128)(2,1)S(1)} %get-tuple-element.32.tokens, bf16[1024,3072]{1,0:T(8,128)(2,1)S(1)} %bitcast.7, bf16[64,1024]{1,0:T(8,128)(2,1)S(1)} %pool.1.after.cells), custom_call_target="tpu_custom_call" | custom-call | flops 1610612736 | tf_op jit(solution)/shard_map/local4/pallas_call | solution.py:374
  28.4 0.0 copy-start
  28.4 0.0 copy-start.1
  28.5 0.0 copy-start.3
  28.5 0.0 collective-permute-done.7.ends0
  28.5 0.1 collective-permute-start.12
  28.6 0.0 collective-permute-done.6.own1
  28.6 0.5 %collective-permute-start.9 = (bf16[64,1024]{1,0:T(8,128)(2,1)S(1)}, bf16[64,1024]{1,0:T(8,128)(2,1)S(1)}, u32[]{:S(2)}, u32[]{:S(2)}) collective-permute-start(bf16[64,1024]{1,0:T(8,128)(2,1)S(1)} %collective-permute-done.6.own1), channel_id=1, source_target_pairs={{0,8},{1,9},{2,10},{3,11},{4,12},{5,13},{6,14},{7,15},{8,0},{9,1},... | collective-permute-start | bytes 393224 | tf_op jit(solution)/shard_map/ppermute | solution.py:299
  29.1 0.1 collective-permute-start.8
  29.2 0.4 %collective-permute-start.10 = (bf16[64,1024]{1,0:T(8,128)(2,1)S(1)}, bf16[64,1024]{1,0:T(8,128)(2,1)S(1)}, u32[]{:S(2)}, u32[]{:S(2)}) collective-permute-start(bf16[64,1024]{1,0:T(8,128)(2,1)S(1)} %collective-permute-done.7.ends0), channel_id=1, source_target_pairs={{0,8},{1,9},{2,10},{3,11},{4,12},{5,13},{6,14},{7,15},{8,0},{9,1},... | collective-permute-start | bytes 393224 | tf_op jit(solution)/shard_map/ppermute | solution.py:299
  29.6 1.6 %near.1.near_pairs = bf16[256,2048]{1,0:T(8,128)(2,1)S(1)} custom-call(s32[4]{0:T(128)S(1)} %pad_add_fusion.refs_0_.place, bf16[64,1024]{1,0:T(8,128)(2,1)S(1)} %collective-permute-done.6.own1, bf16[64,1024]{1,0:T(8,128)(2,1)S(1)} %collective-permute-done.7.ends0, bf16[64,1024]{1,0:T(8,128)(2,1)S(1)} %collective-permute-done.11.ends1, ...), custom_call_target="tpu_custom_call" | custom-call | flops 805306368 | tf_op jit(solution)/shard_map/near/pallas_call | solution.py:438
  31.2 0.1 copy-done.1
  31.3 9.9 %final.1 = bf16[512,1024]{1,0:T(8,128)(2,1)} custom-call(s32[4]{0:T(128)S(1)} %pad_add_fusion.refs_0_.place, s32[2,8]{1,0:T(2,128)S(1)} %copy-done.3, bf16[64,1024]{1,0:T(8,128)(2,1)S(1)} %collective-permute-done.6.own1, bf16[64,1024]{1,0:T(8,128)(2,1)S(1)} %collective-permute-done.8.pair0, bf16[64,1024]{1,0:T(8,128)(2,1)S(1)} %collective-permute-done.9.pair1, ...), custom_call_target="tpu_custom_call" | custom-call | flops 1610612736 | tf_op jit(solution)/shard_map/final/pallas_call | solution.py:450
  (17 shorter events, 0.1 us)
Async XLA Ops:
  2.2 8.6 %collective-permute-start.1 = (bf16[32,1024]{1,0:T(8,128)(2,1)S(1)}, bf16[32,1024]{1,0:T(8,128)(2,1)S(1)}, u32[]{:S(2)}, u32[]{:S(2)}) collective-permute-start(bf16[32,1024]{1,0:T(8,128)(2,1)S(1)} %get-tuple-element.36), channel_id=1, source_target_pairs={{0,2},{1,3},{2,0},{3,1},{4,6},{5,7},{6,4},{7,5},{8,10},{9,11},{10,... | collective-permute-start | bytes 196616 | tf_op jit(solution)/shard_map/ppermute | solution.py:299
  5.3 5.6 %collective-permute-start.2 = (bf16[32,1024]{1,0:T(8,128)(2,1)S(1)}, bf16[32,1024]{1,0:T(8,128)(2,1)S(1)}, u32[]{:S(2)}, u32[]{:S(2)}) collective-permute-start(bf16[32,1024]{1,0:T(8,128)(2,1)S(1)} %get-tuple-element.37), channel_id=1, source_target_pairs={{0,3},{1,2},{2,1},{3,0},{4,7},{5,6},{6,5},{7,4},{8,11},{9,10},{10,... | collective-permute-start | bytes 196616 | tf_op jit(solution)/shard_map/ppermute | solution.py:299
  6.7 4.6 %collective-permute-start = (bf16[32,1024]{1,0:T(8,128)(2,1)S(1)}, bf16[32,1024]{1,0:T(8,128)(2,1)S(1)}, u32[]{:S(2)}, u32[]{:S(2)}) collective-permute-start(bf16[32,1024]{1,0:T(8,128)(2,1)S(1)} %get-tuple-element.33.after), channel_id=1, source_target_pairs={{0,1},{1,0},{2,3},{3,2},{4,5},{5,4},{6,7},{7,6},{8,9},{9,8},{10,11... | collective-permute-start | bytes 196616 | tf_op jit(solution)/shard_map/ppermute | solution.py:299
  6.9 16.9 %slice-start = ((s8[6291456]{0:T(1024)(128)(4,1)}), s8[4194304]{0:T(1024)(128)(4,1)S(1)}, s32[]{:S(2)}) async-start(s8[6291456]{0:T(1024)(128)(4,1)} %bitcast.6), calls=%async_computation | async-start | bytes 8388608
  11.3 12.4 %slice-start.1 = ((s8[6291456]{0:T(1024)(128)(4,1)}), s8[2097152]{0:T(1024)(128)(4,1)S(1)}, s32[]{:S(2)}) async-start(s8[6291456]{0:T(1024)(128)(4,1)} %bitcast.6), calls=%async_computation.1 | async-start | bytes 4194304
  11.4 8.3 %collective-permute-start.5 = (bf16[32,1024]{1,0:T(8,128)(2,1)S(1)}, bf16[32,1024]{1,0:T(8,128)(2,1)S(1)}, u32[]{:S(2)}, u32[]{:S(2)}) collective-permute-start(bf16[32,1024]{1,0:T(8,128)(2,1)S(1)} %get-tuple-element.39.after), channel_id=1, source_target_pairs={{0,6},{1,7},{2,4},{3,5},{4,2},{5,3},{6,0},{7,1},{8,14},{9,15},{10,... | collective-permute-start | bytes 196616 | tf_op jit(solution)/shard_map/ppermute | solution.py:299
  15.0 4.7 %collective-permute-start.4 = (bf16[32,1024]{1,0:T(8,128)(2,1)S(1)}, bf16[32,1024]{1,0:T(8,128)(2,1)S(1)}, u32[]{:S(2)}, u32[]{:S(2)}) collective-permute-start(bf16[32,1024]{1,0:T(8,128)(2,1)S(1)} %get-tuple-element.39.after), channel_id=1, source_target_pairs={{0,2},{1,3},{2,0},{3,1},{4,6},{5,7},{6,4},{7,5},{8,10},{9,11},{10,... | collective-permute-start | bytes 196616 | tf_op jit(solution)/shard_map/ppermute | solution.py:299
  15.0 5.2 %collective-permute-start.3 = (bf16[32,1024]{1,0:T(8,128)(2,1)S(1)}, bf16[32,1024]{1,0:T(8,128)(2,1)S(1)}, u32[]{:S(2)}, u32[]{:S(2)}) collective-permute-start(bf16[32,1024]{1,0:T(8,128)(2,1)S(1)} %get-tuple-element.39.after), channel_id=1, source_target_pairs={{0,4},{1,5},{2,6},{3,7},{4,0},{5,1},{6,2},{7,3},{8,12},{9,13},{10,... | collective-permute-start | bytes 196616 | tf_op jit(solution)/shard_map/ppermute | solution.py:299
  20.2 8.3 %collective-permute-start.11 = (bf16[64,1024]{1,0:T(8,128)(2,1)S(1)}, bf16[64,1024]{1,0:T(8,128)(2,1)S(1)}, u32[]{:S(2)}, u32[]{:S(2)}) collective-permute-start(bf16[64,1024]{1,0:T(8,128)(2,1)S(1)} %pool.1.after.cells), channel_id=1, source_target_pairs={{0,17},{1,16},{2,19},{3,18},{4,21},{5,20},{6,23},{7,22},{8,25},{9,... | collective-permute-start | bytes 393224 | tf_op jit(solution)/shard_map/ppermute | solution.py:299
  22.7 5.7 %collective-permute-start.7 = (bf16[64,1024]{1,0:T(8,128)(2,1)S(1)}, bf16[64,1024]{1,0:T(8,128)(2,1)S(1)}, u32[]{:S(2)}, u32[]{:S(2)}) collective-permute-start(bf16[64,1024]{1,0:T(8,128)(2,1)S(1)} %pool.1.after.cells), channel_id=1, source_target_pairs={{0,16},{1,17},{2,18},{3,19},{4,20},{5,21},{6,22},{7,23},{8,24},{9,... | collective-permute-start | bytes 393224 | tf_op jit(solution)/shard_map/ppermute | solution.py:299
  23.3 5.3 %collective-permute-start.6 = (bf16[64,1024]{1,0:T(8,128)(2,1)S(1)}, bf16[64,1024]{1,0:T(8,128)(2,1)S(1)}, u32[]{:S(2)}, u32[]{:S(2)}) collective-permute-start(bf16[64,1024]{1,0:T(8,128)(2,1)S(1)} %pool.1.after.cells), channel_id=1, source_target_pairs={{0,1},{1,0},{2,3},{3,2},{4,5},{5,4},{6,7},{7,6},{8,9},{9,8},{10,11... | collective-permute-start | bytes 393224 | tf_op jit(solution)/shard_map/ppermute | solution.py:299
  25.0 6.2 %copy-start.2 = (bf16[1024,1024]{1,0:T(8,128)(2,1)S(1)}, bf16[1024,1024]{1,0:T(8,128)(2,1)}, u32[]{:S(2)}) copy-start(bf16[1024,1024]{1,0:T(8,128)(2,1)} %w_out.1) | copy-start | bytes 6291460
  28.4 2.8 %copy-start = (bf16[1024,2048]{1,0:T(8,128)(2,1)S(1)}, bf16[1024,2048]{1,0:T(8,128)(2,1)}, u32[]{:S(2)}) copy-start(bf16[1024,2048]{1,0:T(8,128)(2,1)} %w_kv2.1) | copy-start | bytes 12582916
  28.4 2.9 %copy-start.1 = (bf16[1024,1024]{1,0:T(8,128)(2,1)S(1)}, bf16[1024,1024]{1,0:T(8,128)(2,1)}, u32[]{:S(2)}) copy-start(bf16[1024,1024]{1,0:T(8,128)(2,1)} %w_co.1) | copy-start | bytes 6291460
  28.5 2.9 %copy-start.3 = (s32[2,8]{1,0:T(2,128)S(1)}, s32[2,8]{1,0:T(2,128)}, u32[]{:S(2)}) copy-start(s32[2,8]{1,0:T(2,128)} %lists.1) | copy-start | bytes 196
  28.5 2.7 %collective-permute-start.12 = (bf16[64,1024]{1,0:T(8,128)(2,1)S(1)}, bf16[64,1024]{1,0:T(8,128)(2,1)S(1)}, u32[]{:S(2)}, u32[]{:S(2)}) collective-permute-start(bf16[64,1024]{1,0:T(8,128)(2,1)S(1)} %collective-permute-done.11.ends1), channel_id=1, source_target_pairs={{0,8},{1,9},{2,10},{3,11},{4,12},{5,13},{6,14},{7,15},{8,0},{9,1},... | collective-permute-start | bytes 393224 | tf_op jit(solution)/shard_map/ppermute | solution.py:299
  28.6 2.6 %collective-permute-start.9 = (bf16[64,1024]{1,0:T(8,128)(2,1)S(1)}, bf16[64,1024]{1,0:T(8,128)(2,1)S(1)}, u32[]{:S(2)}, u32[]{:S(2)}) collective-permute-start(bf16[64,1024]{1,0:T(8,128)(2,1)S(1)} %collective-permute-done.6.own1), channel_id=1, source_target_pairs={{0,8},{1,9},{2,10},{3,11},{4,12},{5,13},{6,14},{7,15},{8,0},{9,1},... | collective-permute-start | bytes 393224 | tf_op jit(solution)/shard_map/ppermute | solution.py:299
  29.1 2.1 %collective-permute-start.8 = (bf16[64,1024]{1,0:T(8,128)(2,1)S(1)}, bf16[64,1024]{1,0:T(8,128)(2,1)S(1)}, u32[]{:S(2)}, u32[]{:S(2)}) collective-permute-start(bf16[64,1024]{1,0:T(8,128)(2,1)S(1)} %pool.1.after.cells), channel_id=1, source_target_pairs={{0,8},{1,9},{2,10},{3,11},{4,12},{5,13},{6,14},{7,15},{8,0},{9,1},... | collective-permute-start | bytes 393224 | tf_op jit(solution)/shard_map/ppermute | solution.py:299
  29.2 2.0 %collective-permute-start.10 = (bf16[64,1024]{1,0:T(8,128)(2,1)S(1)}, bf16[64,1024]{1,0:T(8,128)(2,1)S(1)}, u32[]{:S(2)}, u32[]{:S(2)}) collective-permute-start(bf16[64,1024]{1,0:T(8,128)(2,1)S(1)} %collective-permute-done.7.ends0), channel_id=1, source_target_pairs={{0,8},{1,9},{2,10},{3,11},{4,12},{5,13},{6,14},{7,15},{8,0},{9,1},... | collective-permute-start | bytes 393224 | tf_op jit(solution)/shard_map/ppermute | solution.py:299

commit v3 on v2

--- a/solution.py
+++ b/solution.py
@@ -18,7 +18,6 @@
 BF16 = jnp.bfloat16
 
 VM = pl.BlockSpec(memory_space=pltpu.VMEM)
-SM = pl.BlockSpec(memory_space=pltpu.SMEM)
 ANY = pl.BlockSpec(memory_space=pl.ANY)
 FAR = pl.BlockSpec(memory_space=pltpu.HBM)
 
@@ -33,6 +32,10 @@
 
 def dot_t(a, b):
     return lax.dot_general(a, b, (((1,), (1,)), ((), ())), preferred_element_type=F32)
+
+
+def spot():
+    return lax.axis_index("coarse"), lax.axis_index("fine")
 
 
 def call(kernel, outs, in_specs, scratch, limit, flops, moved, name, out_specs=None):
@@ -48,7 +51,7 @@
     )
 
 
-def sums_kernel(chunk, place, starts_far, ends_far, tokens_far, own, send, tokens, roots, acc, root, starts, ends, sem):
+def sums_kernel(chunk, starts_far, ends_far, tokens_far, own, send, tokens, roots, acc, root, starts, ends, sem):
     copies = [
         pltpu.make_async_copy(source, target, sem.at[i])
         for i, (source, target) in enumerate(((starts_far, starts), (ends_far, ends), (tokens_far, tokens)))
@@ -57,8 +60,10 @@
         copy.start()
     rows = tokens.shape[0]
     owned = starts.shape[1]
-    mine = place[0]
-    where_ = place[1] + lax.broadcasted_iota(jnp.int32, (BLK, rows), 1)
+    coarse_index, fine_index = spot()
+    mine = fine_index & 3
+    first_row = (coarse_index * lax.axis_size("fine") + fine_index) * rows
+    where_ = first_row + lax.broadcasted_iota(jnp.int32, (BLK, rows), 1)
     copies[0].wait()
     copies[1].wait()
     members = []
@@ -155,10 +160,10 @@
         target[pl.ds(pl.multiple_of(to, chunk), chunk), columns] = cells[i * chunk : (i + 1) * chunk, :]
 
 
-def near_kernel(chunk, place, own1, ends0, ends1, done, w_qkv, pairs):
+def near_kernel(chunk, own1, ends0, ends1, done, w_qkv, pairs):
     width = w_qkv.shape[0]
     owned = chunk * 4
-    mine = place[0]
+    mine = spot()[1] & 3
     cells = jnp.concatenate([own1[...], ends0[...], ends1[...]], axis=0)
     at = [(mine ^ r) * chunk for r in (1, 3)]
     at += [owned + (mine ^ r ^ 2) * chunk for r in (0, 2, 1, 3)]
@@ -172,18 +177,20 @@
 
 def final_kernel(
     chunk, reach, size, scale, total_rows, head_groups,
-    place, lists, own1, pair0, pair1, side0, side1, done, near_pairs,
+    lists_far, own1, pair0, pair1, side0, side1, done, near_pairs,
     w_qkv, w_co, w_kv2, w_out, *rest,
 ):
-    parts = len(rest) - 8
+    parts = len(rest) - 9
     held = [(p, i) for p, count in enumerate(head_groups) for i in range(count)]
     query, mix, level = (rest[k:parts:3] for k in range(3))
-    out, far_pairs, coarse_query, state, listed, attended, ready, sem = rest[parts:]
-    width = state.shape[1]
+    out, far_pairs, coarse_query, mixes, listed, attended, ready, lists, sem = rest[parts:]
+    lists_copy = pltpu.make_async_copy(lists_far, lists, sem.at[0])
+    lists_copy.start()
+    width = mixes.shape[1]
     owned = chunk * 4
-    mine = place[0]
-    core = place[2]
-    owner = place[3]
+    coarse_index, fine_index = spot()
+    mine = fine_index & 3
+    core = coarse_index & 1
 
     own_at = [owned + (mine ^ r) * chunk for r in (0, 2, 1, 3)]
     pair_at = [(1 - core) * owned + (mine ^ r) * chunk for r in (0, 2, 1, 3)]
@@ -236,16 +243,18 @@
             cells = window(first, span, slice(width + at.start, width + at.stop))
             both = dot(expo, jnp.concatenate([cells, ones], axis=1))
             mixed.append((both[:, :size] / both[:, size:]).astype(BF16))
-        context = dot(jnp.concatenate(mixed, axis=1), w_co[...])
-        state[first : first + BLK, :] = normalize(context).astype(BF16)
-
-    base = (owner - 1) * owned
+        mixes[first : first + BLK, :] = jnp.concatenate(mixed, axis=1)
+
     groups, picks = lists.shape
+    base = total_rows - (coarse_index - 1) * owned
+    lists_copy.wait()
     for n in range(groups):
         for m in range(picks):
-            at = lax.rem(lists[n, m] * KB - base + total_rows, total_rows)
+            at = pl.multiple_of(lax.rem(lists[n, m] * KB + base, total_rows), KB)
             to = (n * picks + m) * KB
-            listed[to : to + KB, :] = state[pl.ds(pl.multiple_of(at, KB), KB), :]
+            listed[to : to + KB, :] = mixes[pl.ds(at, KB), :]
+    listed[...] = normalize(dot(listed[...], w_co[...])).astype(BF16)
+
     here = picks * KB
     ones_here = jnp.ones((here, size), BF16)
     span2 = 2 * size
@@ -254,35 +263,42 @@
         for c in range(0, width, span2)
     ]
 
-    def fine(units):
-        kept = []
-        for n, h in units:
-            part, place_in = held[h]
-            at = slice(place_in * size, (place_in + 1) * size)
-            keys, cells = (c[n * here : (n + 1) * here, h % 2 * size : (h % 2 + 1) * size] for c in second[h // 2])
-            rows = slice(n * QB, (n + 1) * QB)
-            kept.append((part, rows, at, cells, dot_t(query[part][rows, at], keys) * scale))
+    blank = jnp.zeros((here, size), BF16)
+
+    def fine_scores(n, pair):
+        part, place_in = held[2 * pair]
+        both = query[part][n * QB : (n + 1) * QB, place_in * size : (place_in + 2) * size]
+        keys = second[pair][0][n * here : (n + 1) * here, :]
+        first = jnp.concatenate([keys[:, :size], blank], axis=1)
+        other = jnp.concatenate([blank, keys[:, size:]], axis=1)
+        scores = dot_t(both, jnp.concatenate([first, other], axis=0)) * scale
+        return scores[:, :here], scores[:, here:]
+
+    def fine(n):
+        scores = [c for pair in range(HEADS // 2) for c in fine_scores(n, pair)]
+        rows = slice(n * QB, (n + 1) * QB)
+        at = [(part, slice(i * size, (i + 1) * size)) for part, i in held]
         tops = [
-            jnp.maximum(level[part][rows, at], jnp.max(scores, axis=1, keepdims=True))
-            for part, rows, at, cells, scores in kept
+            jnp.maximum(level[part][rows, columns], jnp.max(score, axis=1, keepdims=True))
+            for (part, columns), score in zip(at, scores)
         ]
         boths = []
-        for (part, rows, at, cells, scores), top in zip(kept, tops):
-            expos = jnp.exp2(scores - top[:, :here]).astype(BF16)
+        for h in range(HEADS):
+            expos = jnp.exp2(scores[h] - tops[h][:, :here]).astype(BF16)
+            cells = second[h // 2][1][n * here : (n + 1) * here, h % 2 * size : (h % 2 + 1) * size]
             boths.append(dot(expos, jnp.concatenate([cells, ones_here], axis=1)))
-        for (n, h), (part, rows, at, cells, scores), top, both in zip(units, kept, tops, boths):
-            keep = jnp.exp2(level[part][rows, at] - top)
-            mixed = mix[part][rows, at] * keep + both[:, :size]
-            attended[rows, h * size : (h + 1) * size] = (mixed / (keep + both[:, size:])).astype(BF16)
-
-    units = [(n, h) for h in range(HEADS) for n in range(groups)]
-    for u in range(0, len(units), 8):
-        fine(units[u : u + 8])
+        for h, (part, columns) in enumerate(at):
+            keep = jnp.exp2(level[part][rows, columns] - tops[h])
+            mixed = mix[part][rows, columns] * keep + boths[h][:, :size]
+            attended[rows, h * size : (h + 1) * size] = (mixed / (keep + boths[h][:, size:])).astype(BF16)
+
     copies = []
+    for n in range(groups):
+        fine(n)
     for first in range(0, out.shape[0], BLK):
         some = slice(first, first + BLK)
         ready[some, :] = normalize(dot(attended[some, :], w_out[...])).astype(BF16)
-        copies.append(pltpu.make_async_copy(ready.at[some], out.at[some], sem.at[len(copies)]))
+        copies.append(pltpu.make_async_copy(ready.at[some], out.at[some], sem.at[1 + len(copies)]))
         copies[-1].start()
     for copy in copies:
         copy.wait()
@@ -315,29 +331,25 @@
     size = width // HEADS
     fine_count = lax.axis_size("fine")
     coarse_count = lax.axis_size("coarse")
-    fine_index = lax.axis_index("fine")
     coarse_index = lax.axis_index("coarse")
     owned = seg_start.shape[0]
     chunk = owned // 4
     reach = owned // 2
     scale = math.log2(math.e) / math.sqrt(size)
-    mine = fine_index & 3
+    mine = lax.axis_index("fine") & 3
     big = coarse_count > 4
     far = functools.partial(pltpu.with_memory_space_constraint, memory_space=pltpu.HBM)
     kept = jax.ShapeDtypeStruct if big else pltpu.VMEM
     near = (lambda c: c) if big else functools.partial(pltpu.with_memory_space_constraint, memory_space=pltpu.VMEM)
-    first_row = coarse_index * (rows_here * fine_count) + fine_index * rows_here
-    place = jnp.stack([mine, first_row, coarse_index & 1, coarse_index]).astype(jnp.int32)
-
     own, *send, tokens, roots = call(
-        lambda *refs: sums_kernel(chunk, *refs[:4], refs[4], refs[5:8], *refs[8:]),
+        lambda *refs: sums_kernel(chunk, *refs[:4], refs[4:7], *refs[7:]),
         (
             jax.ShapeDtypeStruct((chunk, width), F32),
             *[jax.ShapeDtypeStruct((chunk, width), BF16)] * 3,
             kept(tokens.shape, BF16),
             jax.ShapeDtypeStruct((2 * chunk, BLK), F32),
         ),
-        [SM, FAR, FAR, FAR],
+        [FAR, FAR, FAR],
         [
             pltpu.VMEM((owned, width), F32),
             pltpu.VMEM((owned, BLK), F32),
@@ -349,9 +361,9 @@
         2 * owned * rows_here * width,
         rows_here * width * 2,
         "sums",
-    )(place, far(seg_start.reshape(1, owned)), far(seg_end.reshape(1, owned)), far(tokens))
-
-    head_groups = (2, 2, 4)
+    )(far(seg_start.reshape(1, owned)), far(seg_end.reshape(1, owned)), far(tokens))
+
+    head_groups = (2, 4, 2)
 
     def local(first, heads, weights, after):
         span = heads * size
@@ -360,8 +372,8 @@
             jax.ShapeDtypeStruct((rows_here, span), F32),
             jax.ShapeDtypeStruct((rows_here, span), F32),
         )
-        cost = 2 * rows_here * width * 3 * span, 0, f"local{first}"
-        if first + heads < HEADS:
+        cost = 2 * rows_here * width * 9 * size, 0, f"local{first}"
+        if first == 0:
             return call(
                 functools.partial(far_kernel, first, heads, size, scale),
                 results,
@@ -394,7 +406,7 @@
         sums, half = add(sums, [swap(half, 0, bit)])
         bit *= 2
     across, beside_half, corner = (swap(half, 0, bit) for bit in (4, 2, 6))
-    sums, part = beside(sums, local(2, 2, w_qkv, half))
+    sums, part = beside(sums, local(2, 4, w_qkv, half))
     parts.extend(part)
     own0 = call(
         pool_kernel,
@@ -430,7 +442,7 @@
         0,
         "rows",
     )(own0, w_qkv)
-    side0, part = beside(side0, local(4, 4, w_qkv, own0))
+    side0, part = beside(side0, local(6, 2, w_qkv, own0))
     side0, (done,) = beside(side0, [done])
     own0 = lax.optimization_barrier((own0, side0))[0]
     parts.extend(part)
@@ -438,19 +450,19 @@
     near_pairs = call(
         functools.partial(near_kernel, chunk),
         jax.ShapeDtypeStruct((2 * owned, 2 * width), BF16),
-        [SM] + [VM] * 5,
+        [VM] * 5,
         [],
         40 if big else 8,
         2 * owned * width * 3 * width,
         0,
         "near",
-    )(place, own1, ends0, ends1, done, w_qkv)
+    )(own1, ends0, ends1, done, w_qkv)
 
     listed_rows = block_lists.shape[0] * block_lists.shape[1] * KB
     return call(
         functools.partial(final_kernel, chunk, reach, size, scale, owned * coarse_count, head_groups),
         jax.ShapeDtypeStruct((rows_here, width), BF16),
-        [SM, SM] + [VM] * (11 + len(parts)),
+        [FAR] + [VM] * (11 + len(parts)),
         [
             pltpu.VMEM((2 * owned, 2 * width), BF16),
             pltpu.VMEM((3 * owned, width), BF16),
@@ -458,7 +470,8 @@
             pltpu.VMEM((listed_rows, width), BF16),
             pltpu.VMEM((rows_here, width), BF16),
             pltpu.VMEM((rows_here, width), BF16),
-            pltpu.SemaphoreType.DMA((rows_here // BLK,)),
+            pltpu.SMEM(block_lists.shape, jnp.int32),
+            pltpu.SemaphoreType.DMA((1 + rows_here // BLK,)),
         ],
         60 if big else 14,
         2 * 2 * owned * width * 3 * width,
@@ -466,7 +479,7 @@
         "final",
         FAR,
     )(
-        place, block_lists, own1, pair0, pair1, side0, side1, done, near_pairs,
+        far(block_lists), own1, pair0, pair1, side0, side1, done, near_pairs,
         w_qkv, near(w_coarse_out), near(w_kv2), near(w_out), *parts,
     )
 

time: 41.6 us -> 39.2 us (0.942)
  Pallas kernels: 26.2 us -> 22.7 us
  waiting for transfers between devices: 0.92 us -> 2.85 us
  starting transfers between devices: 13.7 us -> 13.2 us
    pallas_call x2 -> x1, Pallas kernels: 7.85 us -> 3.85 us  [local(): call(functools.partial(far_kernel, first, heads, size, scale), results, [...]
    pallas_call x1 -> x2, Pallas kernels: 3.4 us -> 5.39 us  [local(): call(kernel, results, [VM, VM, ANY], [], 24 if big else 10, *cost)]
    ppermute x13, waiting for transfers between devices: 0.92 us -> 2.85 us  [swap(): return lax.ppermute(cells, AXES, pairs)]
    pallas_call x1, Pallas kernels: 1.58 us -> 1.02 us  [body(): call(functools.partial(near_kernel, chunk), jax.ShapeDtypeStruct((2 * own...]
    ppermute x13, starting transfers between devices: 13.7 us -> 13.2 us  [swap(): return lax.ppermute(cells, AXES, pairs)]
    pallas_call x1, Pallas kernels: 9.93 us -> 9.4 us  [body(): call(functools.partial(final_kernel, chunk, reach, size, scale, owned * c...]
  transfers between devices with their start and end apart: 13 -> 13, of which waited for: 2 -> 5; matrix products, arithmetic and copies ran while one was open for 0% -> 0% of each run, Pallas kernels for 34% -> 29%
where the time goes in v3:
time: 39.2 us; the launch traced here: 39.1 us
  Pallas kernels  22.7 us (58%)
  starting transfers between devices  13.2 us (34%)
  waiting for transfers between devices  2.85 us (7%)
    ppermute x13, starting transfers between devices, swap(): return lax.ppermute(cells, AXES, pairs)  13.2 us
    pallas_call x1, Pallas kernels, body(): call(functools.partial(final_kernel, chunk, reach, size, scale, owned * c...  9.4 us
    pallas_call x2, Pallas kernels, local(): call(kernel, results, [VM, VM, ANY], [], 24 if big else 10, *cost)  5.39 us
    pallas_call x1, Pallas kernels, local(): call(functools.partial(far_kernel, first, heads, size, scale), results, [...  3.85 us
    ppermute x13, waiting for transfers between devices, swap(): return lax.ppermute(cells, AXES, pairs)  2.85 us
    pallas_call x1, Pallas kernels, body(): call(lambda *refs: sums_kernel(chunk, *refs[:4], refs[4:7], *refs[7:]), (...  1.77 us
    pallas_call x1, Pallas kernels, body(): call(rows_kernel, jax.ShapeDtypeStruct((2 * chunk, 3 * width), BF16), [VM...  1.2 us
    pallas_call x1, Pallas kernels, body(): call(functools.partial(near_kernel, chunk), jax.ShapeDtypeStruct((2 * own...  1.02 us
  transfers between devices with their start and end apart: 13, of which 5 were waited for; matrix products, arithmetic and copies ran while one was open for 0% of the time, Pallas kernels for 29%

profile of v3, /device:TPU:0, one launch (start us, length us, event | category | flops | bytes accessed | tf_op | source)
XLA Modules:
  0.0 39.1 jit_solution(8584007464275017901)
XLA Ops:
  0.0 1.8 %sums.1 = (f32[32,1024]{1,0:T(8,128)S(1)}, bf16[32,1024]{1,0:T(8,128)(2,1)S(1)}, bf16[32,1024]{1,0:T(8,128)(2,1)S(1)}, bf16[32,1024]{1,0:T(8,128)(2,1)S(1)}, bf1...) custom-call(s32[1,128]{1,0:T(1,128)} %bitcast.2, s32[1,128]{1,0:T(1,128)} %bitcast.3, bf16[512,1024]{1,0:T(8,128)(2,1)} %refs_2_.1), custom_call_target="tpu_custom_call" | custom-call | flops 134217728 | bytes 1048576 | tf_op jit(solution)/shard_map/sums/pallas_call | solution.py:344
  1.8 3.1 %collective-permute-start.1 = (bf16[32,1024]{1,0:T(8,128)(2,1)S(1)}, bf16[32,1024]{1,0:T(8,128)(2,1)S(1)}, u32[]{:S(2)}, u32[]{:S(2)}) collective-permute-start(bf16[32,1024]{1,0:T(8,128)(2,1)S(1)} %get-tuple-element.36), channel_id=1, source_target_pairs={{0,2},{1,3},{2,0},{3,1},{4,6},{5,7},{6,4},{7,5},{8,10},{9,11},{10,... | collective-permute-start | bytes 196616 | tf_op jit(solution)/shard_map/ppermute | solution.py:315
  4.9 1.4 %collective-permute-start.2 = (bf16[32,1024]{1,0:T(8,128)(2,1)S(1)}, bf16[32,1024]{1,0:T(8,128)(2,1)S(1)}, u32[]{:S(2)}, u32[]{:S(2)}) collective-permute-start(bf16[32,1024]{1,0:T(8,128)(2,1)S(1)} %get-tuple-element.37), channel_id=1, source_target_pairs={{0,3},{1,2},{2,1},{3,0},{4,7},{5,6},{6,5},{7,4},{8,11},{9,10},{10,... | collective-permute-start | bytes 196616 | tf_op jit(solution)/shard_map/ppermute | solution.py:315
  6.3 0.1 collective-permute-start
  6.4 3.9 %local0.1 = (bf16[512,256]{1,0:T(8,128)(2,1)S(1)}, f32[512,256]{1,0:T(8,128)S(1)}, f32[512,256]{1,0:T(8,128)S(1)}) custom-call(bf16[512,1024]{1,0:T(8,128)(2,1)S(1)} %get-tuple-element.32.tokens, bf16[1024,3072]{1,0:T(8,128)(2,1)} %w_qkv.5, bf16[32,1024]{1,0:T(8,128)(2,1)S(1)} %get-tuple-element.33.after), custom_call_target="tpu_custom_call" | custom-call | flops 1207959552 | tf_op jit(solution)/shard_map/local0/pallas_call | solution.py:377
  10.3 0.0 collective-permute-done.1.rest_1_
  10.3 0.0 collective-permute-done.2.rest_2_
  10.3 0.5 %collective-permute-done.rest_0_ = bf16[32,1024]{1,0:T(8,128)(2,1)S(1)} collective-permute-done((bf16[32,1024]{1,0:T(8,128)(2,1)S(1)}, bf16[32,1024]{1,0:T(8,128)(2,1)S(1)}, u32[]{:S(2)}, u32[]{:S(2)}) %collective-permute-start) | collective-permute-done | bytes 65568 | tf_op jit(solution)/shard_map/ppermute | solution.py:315
  10.9 3.5 %collective-permute-start.5 = (bf16[32,1024]{1,0:T(8,128)(2,1)S(1)}, bf16[32,1024]{1,0:T(8,128)(2,1)S(1)}, u32[]{:S(2)}, u32[]{:S(2)}) collective-permute-start(bf16[32,1024]{1,0:T(8,128)(2,1)S(1)} %get-tuple-element.39.after), channel_id=1, source_target_pairs={{0,6},{1,7},{2,4},{3,5},{4,2},{5,3},{6,0},{7,1},{8,14},{9,15},{10,... | collective-permute-start | bytes 196616 | tf_op jit(solution)/shard_map/ppermute | solution.py:315
  14.4 0.0 collective-permute-start.4
  14.4 0.9 %collective-permute-start.3 = (bf16[32,1024]{1,0:T(8,128)(2,1)S(1)}, bf16[32,1024]{1,0:T(8,128)(2,1)S(1)}, u32[]{:S(2)}, u32[]{:S(2)}) collective-permute-start(bf16[32,1024]{1,0:T(8,128)(2,1)S(1)} %get-tuple-element.39.after), channel_id=1, source_target_pairs={{0,4},{1,5},{2,6},{3,7},{4,0},{5,1},{6,2},{7,3},{8,12},{9,13},{10,... | collective-permute-start | bytes 196616 | tf_op jit(solution)/shard_map/ppermute | solution.py:315
  15.3 3.4 %local2.1 = (bf16[512,512]{1,0:T(8,128)(2,1)S(1)}, f32[512,512]{1,0:T(8,128)S(1)}, f32[512,512]{1,0:T(8,128)S(1)}) custom-call(bf16[512,1024]{1,0:T(8,128)(2,1)S(1)} %get-tuple-element.32.tokens, bf16[1024,3072]{1,0:T(8,128)(2,1)S(1)} %copy-done, bf16[32,1024]{1,0:T(8,128)(2,1)S(1)} %get-tuple-element.39.after), custom_call_target="tpu_custom_call" | custom-call | flops 1207959552 | tf_op jit(solution)/shard_map/local2/pallas_call | solution.py:386
  18.7 0.0 collective-permute-done.5.corner
  18.7 0.8 %collective-permute-done.3.across = bf16[32,1024]{1,0:T(8,128)(2,1)S(1)} collective-permute-done((bf16[32,1024]{1,0:T(8,128)(2,1)S(1)}, bf16[32,1024]{1,0:T(8,128)(2,1)S(1)}, u32[]{:S(2)}, u32[]{:S(2)}) %collective-permute-start.3) | collective-permute-done | bytes 65568 | tf_op jit(solution)/shard_map/ppermute | solution.py:315
  19.6 2.5 %collective-permute-start.11 = (bf16[64,1024]{1,0:T(8,128)(2,1)S(1)}, bf16[64,1024]{1,0:T(8,128)(2,1)S(1)}, u32[]{:S(2)}, u32[]{:S(2)}) collective-permute-start(bf16[64,1024]{1,0:T(8,128)(2,1)S(1)} %pool.1.after.cells), channel_id=1, source_target_pairs={{0,17},{1,16},{2,19},{3,18},{4,21},{5,20},{6,23},{7,22},{8,25},{9,... | collective-permute-start | bytes 393224 | tf_op jit(solution)/shard_map/ppermute | solution.py:315
  22.1 0.5 %collective-permute-start.7 = (bf16[64,1024]{1,0:T(8,128)(2,1)S(1)}, bf16[64,1024]{1,0:T(8,128)(2,1)S(1)}, u32[]{:S(2)}, u32[]{:S(2)}) collective-permute-start(bf16[64,1024]{1,0:T(8,128)(2,1)S(1)} %pool.1.after.cells), channel_id=1, source_target_pairs={{0,16},{1,17},{2,18},{3,19},{4,20},{5,21},{6,22},{7,23},{8,24},{9,... | collective-permute-start | bytes 393224 | tf_op jit(solution)/shard_map/ppermute | solution.py:315
  22.7 0.5 %collective-permute-start.6 = (bf16[64,1024]{1,0:T(8,128)(2,1)S(1)}, bf16[64,1024]{1,0:T(8,128)(2,1)S(1)}, u32[]{:S(2)}, u32[]{:S(2)}) collective-permute-start(bf16[64,1024]{1,0:T(8,128)(2,1)S(1)} %pool.1.after.cells), channel_id=1, source_target_pairs={{0,1},{1,0},{2,3},{3,2},{4,5},{5,4},{6,7},{7,6},{8,9},{9,8},{10,11... | collective-permute-start | bytes 393224 | tf_op jit(solution)/shard_map/ppermute | solution.py:315
  23.2 1.2 %rows.1.done = bf16[64,3072]{1,0:T(8,128)(2,1)S(1)} custom-call(bf16[64,1024]{1,0:T(8,128)(2,1)S(1)} %pool.1.after.cells, bf16[1024,3072]{1,0:T(8,128)(2,1)S(1)} %copy-done), custom_call_target="tpu_custom_call" | custom-call | flops 402653184 | tf_op jit(solution)/shard_map/rows/pallas_call | solution.py:435
  24.4 0.0 copy-start.3
  24.4 2.0 %local6.1 = (bf16[512,256]{1,0:T(8,128)(2,1)S(1)}, f32[512,256]{1,0:T(8,128)S(1)}, f32[512,256]{1,0:T(8,128)S(1)}) custom-call(bf16[512,1024]{1,0:T(8,128)(2,1)S(1)} %get-tuple-element.32.tokens, bf16[1024,3072]{1,0:T(8,128)(2,1)S(1)} %copy-done, bf16[64,1024]{1,0:T(8,128)(2,1)S(1)} %pool.1.after.cells), custom_call_target="tpu_custom_call" | custom-call | flops 1207959552 | tf_op jit(solution)/shard_map/local6/pallas_call | solution.py:386
  26.4 0.0 copy-start.1
  26.4 0.0 copy-start.2
  26.4 0.7 %collective-permute-done.7.ends0 = bf16[64,1024]{1,0:T(8,128)(2,1)S(1)} collective-permute-done((bf16[64,1024]{1,0:T(8,128)(2,1)S(1)}, bf16[64,1024]{1,0:T(8,128)(2,1)S(1)}, u32[]{:S(2)}, u32[]{:S(2)}) %collective-permute-start.7) | collective-permute-done | bytes 131104 | tf_op jit(solution)/shard_map/ppermute | solution.py:315
  27.1 0.0 collective-permute-done.11.ends1
  27.1 0.0 collective-permute-start.12
  27.1 0.5 %collective-permute-done.6.own1 = bf16[64,1024]{1,0:T(8,128)(2,1)S(1)} collective-permute-done((bf16[64,1024]{1,0:T(8,128)(2,1)S(1)}, bf16[64,1024]{1,0:T(8,128)(2,1)S(1)}, u32[]{:S(2)}, u32[]{:S(2)}) %collective-permute-start.6) | collective-permute-done | bytes 131104 | tf_op jit(solution)/shard_map/ppermute | solution.py:315
  27.6 0.5 %collective-permute-start.8 = (bf16[64,1024]{1,0:T(8,128)(2,1)S(1)}, bf16[64,1024]{1,0:T(8,128)(2,1)S(1)}, u32[]{:S(2)}, u32[]{:S(2)}) collective-permute-start(bf16[64,1024]{1,0:T(8,128)(2,1)S(1)} %pool.1.after.cells), channel_id=1, source_target_pairs={{0,8},{1,9},{2,10},{3,11},{4,12},{5,13},{6,14},{7,15},{8,0},{9,1},... | collective-permute-start | bytes 393224 | tf_op jit(solution)/shard_map/ppermute | solution.py:315
  28.1 0.0 collective-permute-start.10
  28.1 1.0 %near.1.near_pairs = bf16[256,2048]{1,0:T(8,128)(2,1)S(1)} custom-call(bf16[64,1024]{1,0:T(8,128)(2,1)S(1)} %collective-permute-done.6.own1, bf16[64,1024]{1,0:T(8,128)(2,1)S(1)} %collective-permute-done.7.ends0, bf16[64,1024]{1,0:T(8,128)(2,1)S(1)} %collective-permute-done.11.ends1, bf16[64,3072]{1,0:T(8,128)(2,1)S(1)} %rows.1.done, ...), custom_call_target="tpu_custom_call" | custom-call | flops 805306368 | tf_op jit(solution)/shard_map/near/pallas_call | solution.py:450
  29.2 0.0 collective-permute-done.8.pair0
  29.2 0.3 collective-permute-done.10.side0
  29.5 9.4 %final.1 = bf16[512,1024]{1,0:T(8,128)(2,1)} custom-call(s32[2,8]{1,0:T(2,128)} %lists_far.1, bf16[64,1024]{1,0:T(8,128)(2,1)S(1)} %collective-permute-done.6.own1, bf16[64,1024]{1,0:T(8,128)(2,1)S(1)} %collective-permute-done.8.pair0, bf16[64,1024]{1,0:T(8,128)(2,1)S(1)} %collective-permute-done.9.pair1, ...), custom_call_target="tpu_custom_call" | custom-call | flops 1610612736 | tf_op jit(solution)/shard_map/final/pallas_call | solution.py:462
  (11 shorter events, 0.1 us)
Async XLA Ops:
  0.0 15.3 %copy-start = (bf16[1024,3072]{1,0:T(8,128)(2,1)S(1)}, bf16[1024,3072]{1,0:T(8,128)(2,1)}, u32[]{:S(2)}) copy-start(bf16[1024,3072]{1,0:T(8,128)(2,1)} %w_qkv.5) | copy-start | bytes 18874372
  1.8 8.5 %collective-permute-start.1 = (bf16[32,1024]{1,0:T(8,128)(2,1)S(1)}, bf16[32,1024]{1,0:T(8,128)(2,1)S(1)}, u32[]{:S(2)}, u32[]{:S(2)}) collective-permute-start(bf16[32,1024]{1,0:T(8,128)(2,1)S(1)} %get-tuple-element.36), channel_id=1, source_target_pairs={{0,2},{1,3},{2,0},{3,1},{4,6},{5,7},{6,4},{7,5},{8,10},{9,11},{10,... | collective-permute-start | bytes 196616 | tf_op jit(solution)/shard_map/ppermute | solution.py:315
  4.9 5.4 %collective-permute-start.2 = (bf16[32,1024]{1,0:T(8,128)(2,1)S(1)}, bf16[32,1024]{1,0:T(8,128)(2,1)S(1)}, u32[]{:S(2)}, u32[]{:S(2)}) collective-permute-start(bf16[32,1024]{1,0:T(8,128)(2,1)S(1)} %get-tuple-element.37), channel_id=1, source_target_pairs={{0,3},{1,2},{2,1},{3,0},{4,7},{5,6},{6,5},{7,4},{8,11},{9,10},{10,... | collective-permute-start | bytes 196616 | tf_op jit(solution)/shard_map/ppermute | solution.py:315
  6.3 4.6 %collective-permute-start = (bf16[32,1024]{1,0:T(8,128)(2,1)S(1)}, bf16[32,1024]{1,0:T(8,128)(2,1)S(1)}, u32[]{:S(2)}, u32[]{:S(2)}) collective-permute-start(bf16[32,1024]{1,0:T(8,128)(2,1)S(1)} %get-tuple-element.33.after), channel_id=1, source_target_pairs={{0,1},{1,0},{2,3},{3,2},{4,5},{5,4},{6,7},{7,6},{8,9},{9,8},{10,11... | collective-permute-start | bytes 196616 | tf_op jit(solution)/shard_map/ppermute | solution.py:315
  10.9 7.8 %collective-permute-start.5 = (bf16[32,1024]{1,0:T(8,128)(2,1)S(1)}, bf16[32,1024]{1,0:T(8,128)(2,1)S(1)}, u32[]{:S(2)}, u32[]{:S(2)}) collective-permute-start(bf16[32,1024]{1,0:T(8,128)(2,1)S(1)} %get-tuple-element.39.after), channel_id=1, source_target_pairs={{0,6},{1,7},{2,4},{3,5},{4,2},{5,3},{6,0},{7,1},{8,14},{9,15},{10,... | collective-permute-start | bytes 196616 | tf_op jit(solution)/shard_map/ppermute | solution.py:315
  14.4 4.3 %collective-permute-start.4 = (bf16[32,1024]{1,0:T(8,128)(2,1)S(1)}, bf16[32,1024]{1,0:T(8,128)(2,1)S(1)}, u32[]{:S(2)}, u32[]{:S(2)}) collective-permute-start(bf16[32,1024]{1,0:T(8,128)(2,1)S(1)} %get-tuple-element.39.after), channel_id=1, source_target_pairs={{0,2},{1,3},{2,0},{3,1},{4,6},{5,7},{6,4},{7,5},{8,10},{9,11},{10,... | collective-permute-start | bytes 196616 | tf_op jit(solution)/shard_map/ppermute | solution.py:315
  14.4 5.2 %collective-permute-start.3 = (bf16[32,1024]{1,0:T(8,128)(2,1)S(1)}, bf16[32,1024]{1,0:T(8,128)(2,1)S(1)}, u32[]{:S(2)}, u32[]{:S(2)}) collective-permute-start(bf16[32,1024]{1,0:T(8,128)(2,1)S(1)} %get-tuple-element.39.after), channel_id=1, source_target_pairs={{0,4},{1,5},{2,6},{3,7},{4,0},{5,1},{6,2},{7,3},{8,12},{9,13},{10,... | collective-permute-start | bytes 196616 | tf_op jit(solution)/shard_map/ppermute | solution.py:315
  19.6 7.5 %collective-permute-start.11 = (bf16[64,1024]{1,0:T(8,128)(2,1)S(1)}, bf16[64,1024]{1,0:T(8,128)(2,1)S(1)}, u32[]{:S(2)}, u32[]{:S(2)}) collective-permute-start(bf16[64,1024]{1,0:T(8,128)(2,1)S(1)} %pool.1.after.cells), channel_id=1, source_target_pairs={{0,17},{1,16},{2,19},{3,18},{4,21},{5,20},{6,23},{7,22},{8,25},{9,... | collective-permute-start | bytes 393224 | tf_op jit(solution)/shard_map/ppermute | solution.py:315
  22.1 5.0 %collective-permute-start.7 = (bf16[64,1024]{1,0:T(8,128)(2,1)S(1)}, bf16[64,1024]{1,0:T(8,128)(2,1)S(1)}, u32[]{:S(2)}, u32[]{:S(2)}) collective-permute-start(bf16[64,1024]{1,0:T(8,128)(2,1)S(1)} %pool.1.after.cells), channel_id=1, source_target_pairs={{0,16},{1,17},{2,18},{3,19},{4,20},{5,21},{6,22},{7,23},{8,24},{9,... | collective-permute-start | bytes 393224 | tf_op jit(solution)/shard_map/ppermute | solution.py:315
  22.7 5.0 %collective-permute-start.6 = (bf16[64,1024]{1,0:T(8,128)(2,1)S(1)}, bf16[64,1024]{1,0:T(8,128)(2,1)S(1)}, u32[]{:S(2)}, u32[]{:S(2)}) collective-permute-start(bf16[64,1024]{1,0:T(8,128)(2,1)S(1)} %pool.1.after.cells), channel_id=1, source_target_pairs={{0,1},{1,0},{2,3},{3,2},{4,5},{5,4},{6,7},{7,6},{8,9},{9,8},{10,11... | collective-permute-start | bytes 393224 | tf_op jit(solution)/shard_map/ppermute | solution.py:315
  24.4 5.1 %copy-start.3 = (bf16[1024,1024]{1,0:T(8,128)(2,1)S(1)}, bf16[1024,1024]{1,0:T(8,128)(2,1)}, u32[]{:S(2)}) copy-start(bf16[1024,1024]{1,0:T(8,128)(2,1)} %w_out.1) | copy-start | bytes 6291460
  26.4 3.1 %copy-start.1 = (bf16[1024,2048]{1,0:T(8,128)(2,1)S(1)}, bf16[1024,2048]{1,0:T(8,128)(2,1)}, u32[]{:S(2)}) copy-start(bf16[1024,2048]{1,0:T(8,128)(2,1)} %w_kv2.1) | copy-start | bytes 12582916
  26.4 3.1 %copy-start.2 = (bf16[1024,1024]{1,0:T(8,128)(2,1)S(1)}, bf16[1024,1024]{1,0:T(8,128)(2,1)}, u32[]{:S(2)}) copy-start(bf16[1024,1024]{1,0:T(8,128)(2,1)} %w_co.1) | copy-start | bytes 6291460
  27.1 2.1 %collective-permute-start.12 = (bf16[64,1024]{1,0:T(8,128)(2,1)S(1)}, bf16[64,1024]{1,0:T(8,128)(2,1)S(1)}, u32[]{:S(2)}, u32[]{:S(2)}) collective-permute-start(bf16[64,1024]{1,0:T(8,128)(2,1)S(1)} %collective-permute-done.11.ends1), channel_id=1, source_target_pairs={{0,8},{1,9},{2,10},{3,11},{4,12},{5,13},{6,14},{7,15},{8,0},{9,1},... | collective-permute-start | bytes 393224 | tf_op jit(solution)/shard_map/ppermute | solution.py:315
  27.6 1.6 %collective-permute-start.9 = (bf16[64,1024]{1,0:T(8,128)(2,1)S(1)}, bf16[64,1024]{1,0:T(8,128)(2,1)S(1)}, u32[]{:S(2)}, u32[]{:S(2)}) collective-permute-start(bf16[64,1024]{1,0:T(8,128)(2,1)S(1)} %collective-permute-done.6.own1), channel_id=1, source_target_pairs={{0,8},{1,9},{2,10},{3,11},{4,12},{5,13},{6,14},{7,15},{8,0},{9,1},... | collective-permute-start | bytes 393224 | tf_op jit(solution)/shard_map/ppermute | solution.py:315
  27.6 1.6 %collective-permute-start.8 = (bf16[64,1024]{1,0:T(8,128)(2,1)S(1)}, bf16[64,1024]{1,0:T(8,128)(2,1)S(1)}, u32[]{:S(2)}, u32[]{:S(2)}) collective-permute-start(bf16[64,1024]{1,0:T(8,128)(2,1)S(1)} %pool.1.after.cells), channel_id=1, source_target_pairs={{0,8},{1,9},{2,10},{3,11},{4,12},{5,13},{6,14},{7,15},{8,0},{9,1},... | collective-permute-start | bytes 393224 | tf_op jit(solution)/shard_map/ppermute | solution.py:315
  28.1 1.3 %collective-permute-start.10 = (bf16[64,1024]{1,0:T(8,128)(2,1)S(1)}, bf16[64,1024]{1,0:T(8,128)(2,1)S(1)}, u32[]{:S(2)}, u32[]{:S(2)}) collective-permute-start(bf16[64,1024]{1,0:T(8,128)(2,1)S(1)} %collective-permute-done.7.ends0), channel_id=1, source_target_pairs={{0,8},{1,9},{2,10},{3,11},{4,12},{5,13},{6,14},{7,15},{8,0},{9,1},... | collective-permute-start | bytes 393224 | tf_op jit(solution)/shard_map/ppermute | solution.py:315
